TPU v7x, 32 devices: a whole 2x2x4 slice. The times are simulated.
32 devices in a mesh: section: 2 (over y), dp: 16 (over z, x, core).
Axes of the slice: x: 2, y: 2, z: 4, core: 2. Of those that a mesh axis runs over, the one named last changes fastest.
Arguments:
- tokens: bfloat16 [2, 16, 2, 128, 768], P(None, 'dp'), may hold values from -6 to 6
- cotangent: bfloat16 [2, 16, 2, 128, 768], P(None, 'dp'), may hold values from -6 to 6
- boxes: int32 [2, 16, 2, 4], P(None, 'dp'), may hold values from 0 to 16, as said below
- timesteps: int32 [2, 16], P(None, 'dp'), may hold values from 0 to 999
- w_ada: float32 [2, 768, 4608], P('section', 'dp'), may hold values from -0.4375 to 0.4375
- w_qkv: float32 [2, 768, 2304], P('section', 'dp'), may hold values from -0.21875 to 0.21875
- w_proj: float32 [2, 768, 768], P('section', 'dp'), may hold values from -0.625 to 0.625
- w_up: float32 [2, 768, 3072], P('section', 'dp'), may hold values from -0.21875 to 0.21875
- w_down: float32 [2, 3072, 768], P('section', 'dp'), may hold values from -0.109375 to 0.109375
Outputs:
- acts: float32 [2, 2, 16, 2, 128, 768], P('section', None, 'dp')
- grad_in: float32 [2, 2, 16, 2, 128, 768], P('section', None, 'dp')
- grad_ada: float32 [2, 768, 4608], P('section', 'dp')
- grad_qkv: float32 [2, 768, 2304], P('section', 'dp')
- grad_proj: float32 [2, 768, 768], P('section', 'dp')
- grad_up: float32 [2, 768, 3072], P('section', 'dp')
- grad_down: float32 [2, 3072, 768], P('section', 'dp')
Inputs may be any that keep to these rules, and one draw needn't show every extreme that they name: boxes hold (top, bottom, left, right) with top < bottom <= 8 and left < right <= 16, so every box holds one patch or more.
All inputs are finite; a program needn't handle non-finite values.
Results may differ from a plain program's by a relative error of at most 0.028.
The roundings to bfloat16 on the way count: a program that leaves them out, or rounds other values in their place, can miss the bound.
Values may be sent and summed in bfloat16 or wider, within the bound.
No kernel may reach another device: no remote copies, remote signals or barrier semaphores. Data moves between devices by JAX's collectives and lax.ppermute only.
A program may use at most 256 MiB of HBM per device.

v0:
```python
from functools import partial
import math

import jax
import jax.numpy as jnp
from jax import lax
from jax.experimental import pallas as pl
from jax.experimental.pallas import tpu as pltpu
from jax.sharding import PartitionSpec as P

HEAD_DIM = 64
GW = 16
LANES = 128
TILE = 64
STEP = 256
EPS = 1e-06
SPARE_BYTES = 10 * 1024 * 1024
EXTRA_BYTES = 2 * 1024 * 1024
f32 = jnp.float32
bf16 = jnp.bfloat16
NN = (((1,), (0,)), ((), ()))
NT = (((1,), (1,)), ((), ()))
TN = (((0,), (0,)), ((), ()))


def mm(a, b, dims=NN):
    return lax.dot_general(a, b, dims, preferred_element_type=f32)


def ln(v):
    centred = v - jnp.mean(v, axis=-1, keepdims=True)
    inv = lax.rsqrt(jnp.mean(centred * centred, axis=-1, keepdims=True) + EPS)
    return centred * inv, inv


def ln_back(normed, inv, grad):
    return inv * (
        grad
        - jnp.mean(grad, axis=-1, keepdims=True)
        - normed * jnp.mean(grad * normed, axis=-1, keepdims=True)
    )


def by_rows(count, body):
    @pl.loop(0, count // STEP)
    def _(i):
        body(pl.ds(pl.multiple_of(i * STEP, STEP), STEP))


def tiles(count, body):
    @pl.loop(0, count // TILE, unroll=True)
    def _(i):
        body(pl.multiple_of(i * TILE, TILE))


def columns(c, j):
    return pl.ds(pl.multiple_of(j * c.width, c.width), c.width)


class Refs(dict):
    __getattr__ = dict.__getitem__


class Names:
    def __getattr__(self, name):
        return name


N = Names()
DP, SECTION = "dp", "section"


class Cfg:
    def __init__(self, frames, patches, width, hidden, blocks):
        self.frames, self.patches, self.width, self.hidden = frames, patches, width, hidden
        self.rows = frames * patches
        self.ratio = hidden // width
        self.blocks = blocks
        self.own = width // blocks
        self.scaling = HEAD_DIM ** (-0.5)


def weight_copies(c, src, dst, sems):
    cuts = (0, 4 * c.own, (4 + c.ratio) * c.own, (4 + 2 * c.ratio) * c.own)
    parts = [pl.ds(a, b - a) for a, b in zip(cuts, cuts[1:])]
    return [
        pltpu.make_async_copy(src.at[:, part, :], dst.at[:, part, :], sems.at[i])
        for i, part in enumerate(parts)
    ]


def square(c, r, j):
    rows = pl.ds(pl.multiple_of(j * c.own, c.own), c.own)
    return r.w[:, rows, :].reshape(c.width, c.width)


def down_block(c, r, j):
    step = c.blocks // c.ratio
    block = r.w[pl.ds(j * step, step), (4 + c.ratio) * c.own :, :]
    return block.reshape(c.width, c.width)


def down_whole(c, r):
    return r.w[:, (4 + c.ratio) * c.own :, :].reshape(c.hidden, c.width)


def fill_given(c, ctl, r):
    patch = lax.broadcasted_iota(jnp.int32, (c.patches, LANES), 0)
    row, col = patch // GW, patch % GW
    for f in range(c.frames):
        top, bottom, left, right = (ctl[1 + 4 * f + i] for i in range(4))
        inside = (row >= top) & (row < bottom) & (col >= left) & (col < right)
        r.given[f * c.patches : (f + 1) * c.patches, :] = jnp.where(inside, 1.0, 0.0)


def pick(c, r, index, given):
    where = slice(index * c.width, (index + 1) * c.width)
    return jnp.where(given, r.mod[0:1, where], r.mod[1:2, where])


def is_given(r, rows):
    return r.given[rows, 0:1] > 0.5


def forward_a(c, r):
    def body(rows):
        given = is_given(r, rows)
        normed, _ = ln(r.x[rows, :].astype(f32))
        r.mixed_a[rows, :] = (normed * (1.0 + pick(c, r, 1, given)) + pick(c, r, 0, given)).astype(
            bf16
        )

    by_rows(c.rows, body)


def forward_qkv(c, r):
    @pl.loop(0, 3, unroll=True)
    def _(j):
        r.packed[:, columns(c, j)] = mm(r.mixed_a[...], square(c, r, j)).astype(bf16)


def halves(pair):
    first = lax.broadcasted_iota(jnp.int32, pair.shape, 1) < HEAD_DIM
    zero = jnp.zeros_like(pair)
    return jnp.concatenate([jnp.where(first, pair, zero), jnp.where(first, zero, pair)], axis=0)


def softmax_rows(scores):
    top = jnp.max(scores, axis=-1, keepdims=True)
    exponent = jnp.exp(scores - top)
    return exponent * (1.0 / jnp.sum(exponent, axis=-1, keepdims=True))


def spatial_tiles(c, body):
    @pl.loop(0, c.width // LANES, unroll=2)
    def _(pair):
        cols = [pl.ds(pl.multiple_of(i * c.width + pair * LANES, LANES), LANES) for i in range(3)]
        for f in range(c.frames):
            body(slice(f * c.patches, (f + 1) * c.patches), cols)


def spatial_merge(c, r):
    def body(rows, cols):
        q, k, v = (r.packed[rows, cols[i]] for i in range(3))
        shares = softmax_rows(mm(halves(q), k, NT) * c.scaling).astype(bf16)
        side = jnp.concatenate([shares[: c.patches], shares[c.patches :]], axis=1)
        r.merged[rows, cols[0]] = mm(side, halves(v)).astype(bf16)

    spatial_tiles(c, body)


def spatial_back(c, r):
    def body(rows, cols):
        q, k, v = (r.packed[rows, cols[i]] for i in range(3))
        q2, k2 = halves(q), halves(k)
        d2 = halves(r.grad_merged[rows, cols[0]])
        soft = softmax_rows(mm(q2, k, NT) * c.scaling)
        grad_shares = mm(d2, v, NT)
        inner = jnp.sum(soft * grad_shares, axis=-1, keepdims=True)
        grad_scores = (soft * (grad_shares - inner)).astype(bf16)
        side = jnp.concatenate([grad_scores[: c.patches], grad_scores[c.patches :]], axis=1)
        r.grad_packed[rows, cols[0]] = (mm(side, k2) * c.scaling).astype(bf16)
        r.grad_packed[rows, cols[1]] = (mm(grad_scores, q2, TN) * c.scaling).astype(bf16)
        r.grad_packed[rows, cols[2]] = mm(soft.astype(bf16), d2, TN).astype(bf16)

    spatial_tiles(c, body)


def fill_heads(c, r):
    lane = lax.broadcasted_iota(jnp.int32, (c.width, LANES), 0) // HEAD_DIM
    col = lax.broadcasted_iota(jnp.int32, (c.width, LANES), 1)
    r.heads_in[...] = jnp.where(lane == col, 1.0, 0.0).astype(bf16)
    col = lax.broadcasted_iota(jnp.int32, (LANES, c.width), 0)
    lane = lax.broadcasted_iota(jnp.int32, (LANES, c.width), 1) // HEAD_DIM
    r.heads_out[...] = jnp.where(lane == col, 1.0, 0.0).astype(bf16)


def head_sums(r, product):
    high = product.astype(bf16)
    low = (product - high.astype(f32)).astype(bf16)
    return mm(high, r.heads_in[...]) + mm(low, r.heads_in[...])


def frame_pairs(c):
    return [(f, g) for f in range(c.frames) for g in range(c.frames)]


def temporal_parts(c, r, ref, rows, part):
    return [
        ref[pl.ds(f * c.patches + rows, TILE), part * c.width : (part + 1) * c.width].astype(f32)
        for f in range(c.frames)
    ]


def temporal_soft(c, r, queries, keys):
    product = jnp.concatenate([queries[f] * keys[g] for f, g in frame_pairs(c)], axis=0)
    scores = head_sums(r, product) * c.scaling
    soft = []
    for f in range(c.frames):
        row = [scores[(f * c.frames + g) * TILE : (f * c.frames + g + 1) * TILE] for g in range(c.frames)]
        top = row[0]
        for entry in row[1:]:
            top = jnp.maximum(top, entry)
        exponent = [jnp.exp(entry - top) for entry in row]
        total = exponent[0]
        for entry in exponent[1:]:
            total = total + entry
        soft += [entry * (1.0 / total) for entry in exponent]
    return soft


def spread(r, columns):
    wide = mm(jnp.concatenate([v.astype(bf16) for v in columns], axis=0), r.heads_out[...])
    return [wide[i * TILE : (i + 1) * TILE] for i in range(len(columns))]


def temporal_merge(c, r):
    def body(rows):
        queries, keys, values = (temporal_parts(c, r, r.packed, rows, i) for i in range(3))
        shares = spread(r, temporal_soft(c, r, queries, keys))
        for f in range(c.frames):
            total = shares[f * c.frames] * values[0]
            for g in range(1, c.frames):
                total = total + shares[f * c.frames + g] * values[g]
            at = f * c.patches + rows
            r.merged[pl.ds(at, TILE), :] = total.astype(bf16)

    tiles(c.patches, body)


def temporal_back(c, r):
    n = c.frames

    def body(rows):
        queries, keys, values = (temporal_parts(c, r, r.packed, rows, i) for i in range(3))
        grads = temporal_parts(c, r, r.grad_merged, rows, 0)
        soft = temporal_soft(c, r, queries, keys)
        product = jnp.concatenate([grads[f] * values[g] for f, g in frame_pairs(c)], axis=0)
        wide = head_sums(r, product)
        grad_shares = [wide[i * TILE : (i + 1) * TILE] for i in range(n * n)]
        grad_scores = []
        for f in range(n):
            inner = soft[f * n] * grad_shares[f * n]
            for g in range(1, n):
                inner = inner + soft[f * n + g] * grad_shares[f * n + g]
            grad_scores += [
                soft[f * n + g] * (grad_shares[f * n + g] - inner) for g in range(n)
            ]
        shares = spread(r, soft)
        scores = spread(r, grad_scores)

        def put(frame, part, value):
            at = frame * c.patches + rows
            r.grad_packed[pl.ds(at, TILE), part * c.width : (part + 1) * c.width] = value.astype(bf16)

        for f in range(n):
            put(f, 0, sum(scores[f * n + g] * keys[g] for g in range(n)) * c.scaling)
            put(f, 1, sum(scores[g * n + f] * queries[g] for g in range(n)) * c.scaling)
            put(f, 2, sum(shares[g * n + f] * grads[g] for g in range(n)))

    tiles(c.patches, body)


def forward_b(c, r):
    r.branch[...] = mm(r.merged[...], square(c, r, 3))

    def body(rows):
        given = is_given(r, rows)
        middle = r.x[rows, :].astype(f32) + pick(c, r, 2, given) * r.branch[rows, :]
        r.middle[rows, :] = middle
        normed, _ = ln(middle)
        r.mixed_b[rows, :] = (normed * (1.0 + pick(c, r, 4, given)) + pick(c, r, 3, given)).astype(
            bf16
        )

    by_rows(c.rows, body)


GELU_A = math.sqrt(2.0 / math.pi)
GELU_B = 0.044715


def forward_mlp(c, r, weight_wait):
    @pl.loop(0, c.ratio, unroll=True)
    def _(j):
        cols = columns(c, j)
        r.hidden[:, cols] = mm(r.mixed_b[...], square(c, r, 4 + j))

        def body(rows):
            h = r.hidden[rows, cols]
            bent = jnp.tanh(GELU_A * (h + GELU_B * (h * h * h)))
            r.active[rows, cols] = (0.5 * h * (1.0 + bent)).astype(bf16)

        by_rows(c.rows, body)

    weight_wait(2)
    r.out_branch[...] = mm(r.active[...], down_whole(c, r))


def forward_end(c, r):
    def body(rows):
        given = is_given(r, rows)
        result = r.middle[rows, :] + pick(c, r, 5, given) * r.out_branch[rows, :]
        r.acts[rows, :] = result
        if N.send in r:
            r.send[rows, :] = result.astype(bf16)

    by_rows(c.rows, body)


def add_sums(c, r, index, given, value):
    cols = slice(index * c.width, (index + 1) * c.width)
    mine = jnp.where(given, value, 0.0)
    rest = jnp.where(given, 0.0, value)
    shape = (value.shape[0] // 8, 8, c.width)
    r.sums[0, :, cols] += jnp.sum(mine.reshape(shape), axis=0)
    r.sums[1, :, cols] += jnp.sum(rest.reshape(shape), axis=0)


def backward_mlp(c, r, gelu_again, put):
    def start(rows):
        given = is_given(r, rows)
        grad = r.grad[rows, :].astype(f32)
        r.grad_out_b[rows, :] = (pick(c, r, 5, given) * grad).astype(bf16)
        add_sums(c, r, 5, given, grad * r.out_branch[rows, :])

    by_rows(c.rows, start)
    put(N.grad_out_b)

    @pl.loop(0, c.ratio, unroll=True)
    def _(j):
        cols = columns(c, j)
        r.temp[...] = mm(r.grad_out_b[...], down_block(c, r, j), NT)

        def body(rows):
            h = r.hidden[rows, cols]
            square_h = h * h
            bent = jnp.tanh(GELU_A * (h + GELU_B * (square_h * h)))
            slope = 0.5 * (1.0 + bent) + 0.5 * h * (1.0 - bent * bent) * (
                GELU_A * (1.0 + 3.0 * GELU_B * square_h)
            )
            r.grad_hidden[rows, cols] = (r.temp[rows, :] * slope).astype(bf16)
            if gelu_again:
                r.active[rows, cols] = (0.5 * h * (1.0 + bent)).astype(bf16)

        by_rows(c.rows, body)

    total = 0.0
    for j in range(c.ratio):
        block = r.grad_hidden[:, j * c.width : (j + 1) * c.width]
        total = total + mm(block, square(c, r, 4 + j), NT)
    r.temp[...] = total


def backward_mid(c, r, mix_again):
    def body(rows):
        given = is_given(r, rows)
        normed, inv = ln(r.middle[rows, :])
        scale = 1.0 + pick(c, r, 4, given)
        if mix_again:
            r.mixed_b[rows, :] = (normed * scale + pick(c, r, 3, given)).astype(bf16)
        grad_mixed = r.temp[rows, :]
        middle = r.grad[rows, :].astype(f32) + ln_back(normed, inv, grad_mixed * scale)
        r.grad_middle[rows, :] = middle
        r.grad_branch[rows, :] = (pick(c, r, 2, given) * middle).astype(bf16)
        add_sums(c, r, 3, given, grad_mixed)
        add_sums(c, r, 4, given, grad_mixed * normed)
        add_sums(c, r, 2, given, middle * r.branch[rows, :])

    by_rows(c.rows, body)
    r.grad_merged[...] = mm(
        r.grad_branch[...], square(c, r, 3), NT
    ).astype(bf16)


def backward_end(c, r, mix_again):
    total = 0.0
    for j in range(3):
        block = r.grad_packed[:, j * c.width : (j + 1) * c.width]
        total = total + mm(block, square(c, r, j), NT)
    r.temp[...] = total

    def body(rows):
        given = is_given(r, rows)
        normed, inv = ln(r.x[rows, :].astype(f32))
        scale = 1.0 + pick(c, r, 1, given)
        if mix_again:
            r.mixed_a[rows, :] = (normed * scale + pick(c, r, 0, given)).astype(bf16)
        grad_mixed = r.temp[rows, :]
        result = r.grad_middle[rows, :] + ln_back(normed, inv, grad_mixed * scale)
        r.grad_in[rows, :] = result
        if N.send in r:
            r.send[rows, :] = result.astype(bf16)
        add_sums(c, r, 0, given, grad_mixed)
        add_sums(c, r, 1, given, grad_mixed * normed)

    by_rows(c.rows, body)


def sizes(c):
    wide, rows = c.width, c.rows
    return dict(
        x=((rows, wide), bf16),
        mod=((2, 6 * wide), f32),
        given=((rows, LANES), f32),
        mixed_a=((rows, wide), bf16),
        packed=((rows, 3 * wide), bf16),
        merged=((rows, wide), bf16),
        branch=((rows, wide), f32),
        middle=((rows, wide), f32),
        mixed_b=((rows, wide), bf16),
        hidden=((rows, c.hidden), f32),
        active=((rows, c.hidden), bf16),
        out_branch=((rows, wide), f32),
        acts=((rows, wide), f32),
        send=((rows, wide), bf16),
        grad=((rows, wide), bf16),
        grad_out_b=((rows, wide), bf16),
        grad_hidden=((rows, c.hidden), bf16),
        temp=((rows, wide), f32),
        grad_middle=((rows, wide), f32),
        grad_branch=((rows, wide), bf16),
        grad_merged=((rows, wide), bf16),
        grad_packed=((rows, 3 * wide), bf16),
        grad_in=((rows, wide), f32),
        sums=((2, 8, 6 * wide), f32),
        grad_mod=((2, 6 * wide), f32),
        heads_in=((wide, LANES), bf16),
        heads_out=((LANES, wide), bf16),
    )


KEPT = (N.packed, N.merged, N.branch, N.middle, N.hidden, N.out_branch)
TERMS = (
    N.mixed_a,
    N.grad_packed,
    N.merged,
    N.grad_branch,
    N.mixed_b,
    N.grad_hidden,
    N.active,
    N.grad_out_b,
)


class Traffic:
    def __init__(self, sems):
        self.sems, self.used, self.pending = sems, 0, {}

    def start(self, name, src, dst):
        copy = pltpu.make_async_copy(src, dst, self.sems.at[self.used])
        self.used += 1
        copy.start()
        self.pending[name] = copy

    def wait(self, name):
        if name in self.pending:
            self.pending.pop(name).wait()

    def drain(self):
        for name in list(self.pending):
            self.wait(name)


def run_forward(c, r, t, temporal, put, weight_wait):
    t.wait(N.mod)
    t.wait(N.x)
    forward_a(c, r)
    put(N.mixed_a)
    weight_wait(0)
    forward_qkv(c, r)
    put(N.packed)
    if temporal:
        fill_heads(c, r)
        temporal_merge(c, r)
    else:
        spatial_merge(c, r)
    put(N.merged)
    forward_b(c, r)
    put(N.branch)
    put(N.middle)
    put(N.mixed_b)
    weight_wait(1)
    forward_mlp(c, r, weight_wait)
    put(N.hidden)
    put(N.active)
    put(N.out_branch)
    forward_end(c, r)
    put(N.acts)
    put(N.send)


def spatial_forward_kernel(c, micro, names, refs):
    h = Refs(names_hbm(names, refs))
    r = h.vmem
    first = N.near in h
    r[N.w] = h.near if first else h.w
    copies = weight_copies(c, h.w, h.near, r.wsem) if first else []
    for copy in copies:
        copy.start()

    @pl.when(h.ctl[0] == 0)
    def _():
        t = Traffic(r.sems)
        t.start(N.x, h.x.at[micro], r.x)
        t.start(N.mod, h.mod.at[micro], r.mod)
        fill_given(c, h.ctl, r)

        def put(name):
            if name in KEPT or name == N.send:
                t.start(name, r[name], h[name])
            elif name == N.acts:
                t.start(name, r.acts, h.acts.at[micro])

        def weight_wait(part):
            if first:
                copies[part].wait()

        run_forward(c, r, t, False, put, weight_wait)
        t.drain()

    if first:

        @pl.when(h.ctl[0] != 0)
        def _():
            for copy in copies:
                copy.wait()


def temporal_kernel(c, micro, names, refs):
    h = Refs(names_hbm(names, refs))
    r = h.vmem

    @pl.when(h.ctl[0] == 1)
    def _():
        t = Traffic(r.sems)
        r.update(x=h.x, w=h.w)
        t.start(N.mod, h.mod.at[micro], r.mod)
        t.start(N.grad, h.cot.at[micro], r.grad)
        fill_given(c, h.ctl, r)
        forward = Refs({k: v for k, v in r.items() if k != N.send})
        put = partial(put_backward, c, micro, h, r, t)
        run_forward(
            c,
            forward,
            t,
            True,
            lambda name: name == N.send or put(name),
            lambda part: None,
        )
        t.wait(N.grad)
        r.sums[...] = jnp.zeros_like(r.sums)
        backward_first(c, r, t, True, put)
        backward_second(c, r, t, True, put)
        t.drain()


def put_backward(c, micro, h, r, t, name):
    if name == N.send:
        if N.send in h:
            t.start(N.send, r.send, h.send)
    elif name in (N.acts, N.grad_in):
        t.start(name, r[name], h[name].at[micro])
    elif name in (N.late_sums, N.early_sums):
        early = 2 * c.width
        cols = pl.ds(0, early) if name == N.early_sums else pl.ds(early, 2 * early)
        t.start(name, r.grad_mod.at[:, cols], h.grad_mod.at[micro, :, cols])
    elif name in TERMS:
        t.start(name, r[name], h[name].at[pl.ds(micro * c.rows, c.rows), :])


def backward_first(c, r, t, temporal, put):
    backward_mlp(c, r, not temporal, put)
    put(N.grad_hidden)
    if not temporal:
        put(N.active)
    t.wait(N.middle)
    t.wait(N.branch)
    backward_mid(c, r, not temporal)
    put(N.grad_branch)
    if not temporal:
        put(N.mixed_b)
    put_sums(c, r, 2, 6)
    put(N.late_sums)


def backward_second(c, r, t, temporal, put):
    if temporal:
        temporal_back(c, r)
    else:
        spatial_back(c, r)
    put(N.grad_packed)
    t.wait(N.x)
    backward_end(c, r, not temporal)
    if not temporal:
        put(N.mixed_a)
    put(N.send)
    put(N.grad_in)
    put_sums(c, r, 0, 2)
    put(N.early_sums)


def put_sums(c, r, first, last):
    cols = slice(first * c.width, last * c.width)
    r.grad_mod[:, cols] = jnp.sum(r.sums[:, :, cols], axis=1)


def spatial_backward_kernel(c, micro, names, refs):
    h = Refs(names_hbm(names, refs))
    r = h.vmem

    @pl.when(h.ctl[0] == 0)
    def _():
        t = Traffic(r.sems)
        r.update(grad=h.grad, w=h.w)
        t.start(N.mod, h.mod.at[micro], r.mod)
        t.start(N.out_branch, h.out_branch, r.out_branch)
        t.start(N.hidden, h.hidden, r.hidden)
        t.start(N.middle, h.middle, r.middle)
        t.start(N.branch, h.branch, r.branch)
        t.start(N.packed, h.packed, r.packed)
        t.start(N.kept, h.kept, r.merged)
        t.start(N.x, h.x.at[micro], r.x)
        fill_given(c, h.ctl, r)
        r.sums[...] = jnp.zeros_like(r.sums)
        for name in (N.mod, N.out_branch, N.hidden):
            t.wait(name)
        put = partial(put_backward, c, micro, h, r, t)
        backward_first(c, r, t, False, put)
        t.wait(N.packed)
        t.wait(N.kept)
        put(N.merged)
        backward_second(c, r, t, False, put)
        t.drain()


def spatial_first_kernel(c, micro, names, refs):
    h = Refs(names_hbm(names, refs))
    r = h.vmem

    @pl.when(h.ctl[0] == 0)
    def _():
        t = Traffic(r.sems)
        r.update(grad=h.grad, w=h.w)
        t.start(N.mod, h.mod.at[micro], r.mod)
        t.start(N.out_branch, h.out_branch, r.out_branch)
        t.start(N.hidden, h.hidden, r.hidden)
        t.start(N.middle, h.middle, r.middle)
        t.start(N.branch, h.branch, r.branch)
        t.start(N.kept, h.kept, r.merged)
        fill_given(c, h.ctl, r)
        r.sums[...] = jnp.zeros_like(r.sums)
        for name in (N.mod, N.out_branch, N.hidden):
            t.wait(name)
        put = partial(put_backward, c, micro, h, r, t)
        t.wait(N.kept)
        put(N.merged)
        backward_first(c, r, t, False, put)
        t.start(N.grad_middle, r.grad_middle, h.grad_middle)
        t.start(N.grad_merged, r.grad_merged, h.grad_merged)
        t.drain()


def spatial_second_kernel(c, micro, names, refs):
    h = Refs(names_hbm(names, refs))
    r = h.vmem

    @pl.when(h.ctl[0] == 0)
    def _():
        t = Traffic(r.sems)
        r.update(w=h.w)
        for name in (N.packed, N.grad_merged):
            t.start(name, h[name], r[name])
        t.start(N.x, h.x.at[micro], r.x)
        t.start(N.mod, h.mod.at[micro], r.mod)
        t.start(N.grad_middle, h.grad_middle, r.grad_middle)
        fill_given(c, h.ctl, r)
        r.sums[...] = jnp.zeros_like(r.sums)
        for name in (N.packed, N.grad_merged, N.grad_middle, N.mod):
            t.wait(name)
        put = partial(put_backward, c, micro, h, r, t)
        backward_second(c, r, t, False, put)
        t.drain()


def names_hbm(names, refs):
    outer, inner = names
    found = dict(zip(outer, refs[: len(outer)], strict=True))
    found[N.vmem] = Refs(zip(inner, refs[len(outer) :], strict=True))
    return found


def vmem_bytes(scratch):
    sizes = [
        math.prod(v.shape) * jnp.dtype(v.dtype).itemsize
        for v in scratch
        if v.memory_space == pltpu.VMEM
    ]
    return sum(sizes) + SPARE_BYTES


def call(c, kernel, micro, operands, news, alias, scratch, flops):
    ins = list(operands)
    outs = list(alias) + list(news)
    shapes = [pltpu.HBM(operands[n].shape, operands[n].dtype) for n in alias]
    shapes += [
        (pltpu.VMEM if n == N.near else jax.ShapeDtypeStruct if n == N.send else pltpu.HBM)(*news[n])
        for n in news
    ]
    table = sizes(c)
    inner = {n: pltpu.VMEM(*table[n]) for n in scratch}
    if N.near in news:
        inner[N.wsem] = pltpu.SemaphoreType.DMA((3,))
    inner[N.sems] = pltpu.SemaphoreType.DMA((32,))
    in_names = [n if n not in alias else "_" + n for n in ins]
    names = (in_names + outs, list(inner))
    places = {N.ctl: pltpu.SMEM, N.grad: pltpu.VMEM}
    if N.near not in news:
        places[N.w] = pltpu.VMEM
    if kernel is temporal_kernel:
        places[N.x] = pltpu.VMEM
    got = pl.pallas_call(
        lambda *refs: kernel(c, micro, names, refs),
        out_shape=shapes,
        in_specs=[
            pl.BlockSpec(memory_space=places.get(n, pl.ANY)) for n in ins
        ],
        out_specs=[
            pl.BlockSpec(memory_space=pltpu.VMEM if n == N.near else pl.ANY) for n in outs
        ],
        scratch_shapes=list(inner.values()),
        input_output_aliases={ins.index(n): i for i, n in enumerate(alias)},
        compiler_params=pltpu.CompilerParams(
            vmem_limit_bytes=vmem_bytes(inner.values()) + EXTRA_BYTES * (kernel is temporal_kernel)
        ),
        cost_estimate=pl.CostEstimate(flops=flops, bytes_accessed=20_000_000, transcendentals=0),
    )(*operands.values())
    return dict(zip(outs, got, strict=True))


FIRST = (N.merged, N.grad_branch, N.mixed_b, N.grad_hidden, N.active, N.grad_out_b)
SECOND = (N.mixed_b, N.grad_hidden, N.mixed_a, N.grad_packed)
LEAD = 2


def group_rows(c):
    return ((c.ratio + 1) * c.own, (c.ratio - LEAD + 3) * c.own, LEAD * c.own)


def gradients_kernel(c, ring, order, place, *refs):
    made = (0, 2) if order == FIRST else (1,)
    each = (4, 4, 2) if ring else (1, 1, 1)
    count, outs = len(order), sum(each[g] for g in made)
    held = Refs(zip(order, refs[count + outs : 2 * count + outs], strict=True))
    turned, slots, in_sems, out_sems = refs[2 * count + outs :]
    sources = dict(zip(order, refs, strict=False))
    lead = LEAD * c.width
    needed = pl.ds(0, lead) if order == FIRST else pl.ds(lead, c.hidden - lead)
    sources[N.grad_hidden] = sources[N.grad_hidden].at[:, needed]
    copies = {
        n: pltpu.make_async_copy(sources[n], held[n], in_sems.at[i]) for i, n in enumerate(order)
    }
    for copy in copies.values():
        copy.start()
    own, step, line = c.own, c.blocks // c.ratio, c.blocks // 4
    out, at = {}, count
    for g in made:
        out[g] = refs[at : at + each[g]]
        at += each[g]

    def puts(slot, group, j, tall=False):
        ref = slots.at[slot]
        if tall:
            ref = ref.reshape(step, c.ratio * own, c.width)
        if not ring:
            rows = pl.ds(j * step, step) if tall else pl.ds(0, c.blocks)
            part = pl.ds(0, c.ratio * own) if tall else pl.ds(j * own, own)
            yield pltpu.make_async_copy(ref, out[group][0].at[rows, part, :], out_sems.at[slot, 0])
            return
        if tall:
            ref = ref.reshape(2, 2, c.ratio * own, c.width)
            places, rows = j, pl.ds(0, c.ratio * own)
        else:
            ref = ref.reshape(line, 2, 2, own, c.width)
            places, rows = slice(None), pl.ds(j * own, own)
        for i, (x, core) in enumerate(((0, 0), (1, 0), (0, 1), (1, 1))):
            at = ((place[0] + x) % 2, (place[1] + core) % 2)
            src = ref.at[at] if tall else ref.at[:, at[0], at[1]]
            if group == 2:
                dst = out[group][core].at[places, x, rows, :]
            else:
                dst = out[group][i].at[places, rows, :]
            yield pltpu.make_async_copy(src, dst, out_sems.at[slot, i])

    def product(left, right, dims, *target):
        slots[target[0]] = mm(left, right, dims).astype(bf16).reshape(slots.shape[1:])
        for copy in puts(*target):
            copy.start()

    rest = c.ratio - LEAD
    if order == FIRST:
        last = c.ratio + LEAD
        copies[N.merged].wait()
        copies[N.grad_branch].wait()
        product(held.merged[...], held.grad_branch[...], TN, last, 0, c.ratio)
        copies[N.mixed_b].wait()
        turned[...] = held.mixed_b[...].T
        copies[N.grad_hidden].wait()

        @pl.loop(0, LEAD)
        def _(j):
            product(turned[...], held.grad_hidden[:, columns(c, j)], NN, c.ratio + j, 2, j)

        copies[N.active].wait()
        copies[N.grad_out_b].wait()

        @pl.loop(0, c.ratio)
        def _(j):
            product(held.active[:, columns(c, j)], held.grad_out_b[...], TN, j, 0, j, True)

        targets = [(j, 0, j, True) for j in range(c.ratio)] + [(last, 0, c.ratio)]
        targets += [(c.ratio + j, 2, j) for j in range(LEAD)]
    else:
        copies[N.mixed_b].wait()
        turned[...] = held.mixed_b[...].T
        copies[N.grad_hidden].wait()

        @pl.loop(0, rest)
        def _(j):
            product(turned[...], held.grad_hidden[:, columns(c, j)], NN, j, 1, j)

        copies[N.mixed_a].wait()
        turned[...] = held.mixed_a[...].T
        copies[N.grad_packed].wait()

        @pl.loop(0, 3)
        def _(j):
            product(turned[...], held.grad_packed[:, columns(c, j)], NN, rest + j, 1, rest + j)

        targets = [(j, 1, j) for j in range(rest + 3)]
    for target in targets:
        for copy in puts(*target):
            copy.wait()


def weight_gradients(c, ring, order, place, terms):
    made = (0, 2) if order == FIRST else (1,)
    jobs = c.ratio + LEAD + 1 if order == FIRST else c.ratio - LEAD + 3
    shapes = [terms[n].shape for n in order]
    lead = LEAD * c.width
    at = order.index(N.grad_hidden)
    shapes[at] = (shapes[at][0], lead if order == FIRST else c.hidden - lead)
    line, each = (c.blocks // 4, (4, 4, 2)) if ring else (c.blocks, (1, 1, 1))
    out = []
    for group in made:
        shape = (line, group_rows(c)[group], c.width)
        if ring and group == 2:
            shape = (line, 2) + shape[1:]
        plain = jax.ShapeDtypeStruct(shape, bf16)
        if ring and group == 0:
            out += [pltpu.HBM(shape, bf16), plain, pltpu.HBM(shape, bf16), plain]
        else:
            out += [plain] * each[group]
    scratch = [pltpu.VMEM(s, bf16) for s in shapes] + [
        pltpu.VMEM((c.width, shapes[0][0]), bf16),
        pltpu.VMEM((jobs, c.blocks, c.own, c.width), bf16),
        pltpu.SemaphoreType.DMA((len(order),)),
        pltpu.SemaphoreType.DMA((jobs, 4)),
    ]
    got = pl.pallas_call(
        partial(gradients_kernel, c, ring, order),
        out_shape=out,
        in_specs=[pl.BlockSpec(memory_space=pltpu.SMEM)]
        + [pl.BlockSpec(memory_space=pl.ANY)] * len(order),
        out_specs=[pl.BlockSpec(memory_space=pl.ANY)] * len(out),
        scratch_shapes=scratch,
        compiler_params=pltpu.CompilerParams(vmem_limit_bytes=vmem_bytes(scratch)),
        cost_estimate=pl.CostEstimate(
            flops=2 * shapes[0][0] * c.width * c.width * jobs,
            bytes_accessed=12_000_000,
            transcendentals=0,
        ),
    )(place, *[pltpu.with_memory_space_constraint(terms[n], pltpu.HBM) for n in order])
    return [got[: each[0]], got[each[0] :]] if order == FIRST else [got]


def add(*parts):
    total = parts[0].astype(f32)
    for part in parts[1:]:
        total = total + part.astype(f32)
    return total


LINE = (3, 2, 1)


def line_terms(z, *parts):
    def at(part, k):
        return lax.dynamic_index_in_dim(part, z ^ k, 0, keepdims=False)

    return [add(*[at(part, k) for part in parts]).astype(bf16) for k in (0,) + LINE]


def line_swap(terms):
    return terms[:1] + [swap(term, 4 * k) for term, k in zip(terms[1:], LINE)]


def ring_sums(first, second, z, sums):
    meet = lax.optimization_barrier
    (near0, far0, *core0), (both2, core2) = first
    far0 = add(far0, swap(core0[1], 1)).astype(bf16)
    terms2 = line_terms(z, both2, swap(core2, 1))

    far0, terms2, near_core0 = meet((far0, terms2, core0[0]))
    group1, small = second((far0, terms2))
    far0, terms2 = swap(far0, 2), line_swap(terms2)
    core0 = swap(near_core0, 1)

    far0, terms2, core0, (near1, far1, *core1), small = meet((far0, terms2, core0, group1, small))
    far1 = add(far1, swap(core1[1], 1)).astype(bf16)
    sum2 = add(*terms2)
    other2, sum2 = sum2[1].astype(bf16), sum2[0]
    far0, far1, other2, sum2, small = meet((far0, far1, other2, sum2, small))
    terms0 = line_swap(line_terms(z, near0, core0, far0))
    far1 = swap(far1, 2)
    core1 = swap(core1[0], 1)
    small = gather_step(gather_step(sums(small)[None], 8), 4)

    terms0, far1, core1, small = meet((terms0, far1, core1, small))
    terms1 = line_swap(line_terms(z, near1, core1, far1))
    sum2 = sum2 + swap(other2, 2).astype(f32)
    small = gather_step(gather_step(small, 2), 1)
    return add(*terms0), add(*terms1), sum2, small


def swap(block, distance):
    count = lax.axis_size(DP)
    return lax.ppermute(block, DP, [(i, i ^ distance) for i in range(count)])


def gather_small(block):
    count = lax.axis_size(DP)
    if count & (count - 1):
        return lax.all_gather(block, DP, axis=0, tiled=False)
    held, distance = block[None], count // 2
    while distance:
        held = gather_step(held, distance)
        distance //= 2
    return held


def gather_step(held, distance):
    other = swap(held, distance)
    lower = (lax.axis_index(DP) & distance) == 0
    pair = [jnp.where(lower, held, other), jnp.where(lower, other, held)]
    return jnp.stack(pair, axis=1).reshape((-1,) + held.shape[1:])


def scatter_small(blocks):
    count = lax.axis_size(DP)
    if count & (count - 1):
        return lax.psum_scatter(blocks, DP, scatter_dimension=0, tiled=False)
    mine = lax.axis_index(DP)
    distance = 1
    while distance < count:
        low, high = blocks[0::2], blocks[1::2]
        upper = (mine & distance) != 0
        other = swap(jnp.where(upper, low, high), distance)
        blocks = jnp.where(upper, high, low) + other
        distance *= 2
    return blocks[0]


def embed_columns(steps, index, width):
    half = width // 2
    place = (index % half).astype(f32)
    frequency = jnp.exp(-math.log(10000.0) * place / half)
    angles = steps.astype(f32)[:, None] * frequency[None, :]
    wave = jnp.where((index < half)[None, :], jnp.cos(angles), jnp.sin(angles))
    return jax.nn.silu(wave).astype(bf16)


def by_blocks(w, own, width):
    return jnp.concatenate([w[:, at : at + width] for at in range(0, w.shape[1], width)])


def in_vmem(block):
    return pltpu.with_memory_space_constraint(block, pltpu.VMEM)


def from_blocks(blocks, own, width):
    starts = range(0, blocks.shape[0], own)
    return jnp.concatenate([blocks[at : at + own] for at in starts], axis=1)


def local(tokens, cotangent, boxes, timesteps, w_ada, w_qkv, w_proj, w_up, w_down):
    section = lax.axis_index(SECTION)
    group = lax.axis_size(DP)
    micro_count, _, frames, patches, width = tokens.shape
    hidden = w_up.shape[2]
    rows = frames * patches
    own = width // group
    ratio = hidden // width
    direct = own % 16 == 0 and group % ratio == 0
    ring = direct and group == 16 and ratio == 4
    c = Cfg(frames, patches, width, hidden, group if direct else ratio)

    shard = jnp.concatenate(
        [
            by_blocks(w_qkv[0].astype(bf16), own, width),
            w_proj[0].astype(bf16),
            by_blocks(w_up[0].astype(bf16), own, width),
            w_down[0].astype(bf16),
        ],
        axis=0,
    )
    weights = lax.all_gather(shard, DP, axis=0, tiled=False)
    squares = 4 + ratio
    if not direct:
        weights = jnp.concatenate(
            [
                weights[:, i * own : (i + 1) * own].reshape(c.blocks, c.own, width)
                for i in range(squares)
            ]
            + [weights[:, squares * own :].reshape(c.blocks, ratio * c.own, width)],
            axis=1,
        )

    start = lax.axis_index(DP) * own
    index = start + jnp.arange(own, dtype=jnp.int32)
    steps = gather_small(timesteps.reshape(micro_count))
    steps = jnp.concatenate([jnp.zeros((group, 1), steps.dtype), steps], axis=1)
    embed = embed_columns(steps.reshape(-1), index, width)
    modulation = jnp.dot(embed, w_ada[0].astype(bf16), preferred_element_type=f32)
    modulation = scatter_small(modulation.reshape(group, 1 + micro_count, 6 * width))
    modulation = jnp.stack(
        [jnp.stack([modulation[0], modulation[1 + m]]) for m in range(micro_count)]
    )
    ctl = [
        jnp.concatenate([section.astype(jnp.int32)[None], boxes[m].reshape(-1)])
        for m in range(micro_count)
    ]

    tokens = tokens.reshape(micro_count, rows, width)
    cotangent = cotangent.reshape(micro_count, rows, width)
    whole = ((micro_count, rows, width), f32)
    one = ((rows, width), bf16)
    flops = 2 * rows * width * width * (4 + 2 * ratio)
    table = sizes(c)

    forward_names = [
        N.x, N.mod, N.given, N.mixed_a, N.packed, N.merged, N.branch, N.middle, N.mixed_b,
        N.hidden, N.active, N.out_branch, N.acts, N.send,
    ]
    back_names = [
        N.grad, N.grad_out_b, N.grad_hidden, N.temp, N.grad_middle, N.grad_branch, N.grad_merged,
        N.grad_packed, N.grad_in, N.sums, N.grad_mod,
    ]
    kept, received = [], []
    acts = None
    for m in range(micro_count):
        operands = dict(ctl=ctl[m], x=tokens, mod=modulation, w=weights)
        if m == 0:
            operands[N.w] = pltpu.with_memory_space_constraint(weights, pltpu.HBM)
        news = dict(send=one, **{n: table[n] for n in KEPT})
        if acts is None:
            news.update(acts=whole, near=(weights.shape, bf16))
        else:
            operands[N.acts] = acts
        alias = [N.acts] if acts is not None else []
        got = call(c, spatial_forward_kernel, m, operands, news, alias, forward_names, flops)
        acts = got[N.acts]
        if m == 0:
            weights = in_vmem(got[N.near])
        kept.append(got)
        received.append(in_vmem(lax.ppermute(got[N.send], SECTION, [(0, 1)])))

    shared = None
    grads = []
    for m in range(micro_count):
        operands = dict(
            ctl=ctl[m], x=received[m], mod=modulation, w=weights, cot=cotangent, acts=acts
        )
        news = dict(send=one)
        alias = [N.acts]
        if shared is None:
            news[N.grad_in] = whole
            news[N.grad_mod] = ((micro_count, 2, 6 * width), f32)
            for n in TERMS:
                news[n] = ((micro_count * rows, table[n][0][1]), bf16)
        else:
            operands.update(shared)
            alias += list(shared)
        names = forward_names + back_names + [N.heads_in, N.heads_out]
        got = call(c, temporal_kernel, m, operands, news, alias, names, 3 * flops)
        acts = got[N.acts]
        shared = {n: got[n] for n in (N.grad_in, N.grad_mod) + TERMS}
        grads.append(in_vmem(lax.ppermute(got[N.send], SECTION, [(1, 0)])))

    dp_index = lax.axis_index(DP)
    place = jnp.stack([dp_index // 2 % 2, dp_index % 2]).astype(jnp.int32)
    names = [n for n in forward_names if n not in (N.acts, N.send)] + back_names
    firsts = (N.grad_mod, N.grad_out_b, N.grad_hidden, N.active, N.mixed_b, N.grad_branch, N.merged)
    seconds = (N.grad_in, N.grad_mod, N.grad_packed, N.mixed_a)

    def operands_of(m, own_names, **more):
        got = dict(ctl=ctl[m], mod=modulation, w=weights, **more)
        for n in own_names:
            got[N.kept if n == N.merged else n] = kept[m][n]
        return got

    last = micro_count - 1
    for m in range(last):
        operands = operands_of(m, KEPT, grad=grads[m], x=tokens)
        operands.update(shared)
        shared = call(
            c, spatial_backward_kernel, m, operands, {}, list(shared), names, 2 * flops
        )
    ours = (N.out_branch, N.hidden, N.middle, N.branch, N.merged)
    operands = operands_of(last, ours, grad=grads[last])
    operands.update({n: shared[n] for n in firsts})
    news = dict(grad_middle=table[N.grad_middle], grad_merged=one)
    first_names = [
        N.mod, N.given, N.out_branch, N.hidden, N.middle, N.branch, N.merged, N.mixed_b, N.active,
        N.grad_out_b, N.grad_hidden, N.temp, N.grad_middle, N.grad_branch, N.grad_merged, N.sums,
        N.grad_mod,
    ]
    got = call(c, spatial_first_kernel, last, operands, news, firsts, first_names, 4 * flops // 3)
    shared.update({n: got[n] for n in firsts})
    between = {n: got[n] for n in news}
    first = weight_gradients(c, ring, FIRST, place, shared)

    def second(after):
        (grad_middle, grad_merged), _ = lax.optimization_barrier((tuple(between.values()), after))
        operands = operands_of(
            last, (N.packed,), x=tokens, grad_middle=grad_middle, grad_merged=grad_merged
        )
        operands.update({n: shared[n] for n in seconds})
        second_names = [
            N.x, N.mod, N.given, N.packed, N.mixed_a, N.temp, N.grad_middle, N.grad_merged,
            N.grad_packed, N.grad_in, N.sums, N.grad_mod,
        ]
        got = call(
            c, spatial_second_kernel, last, operands, {}, seconds, second_names, 2 * flops // 3
        )
        shared.update({n: got[n] for n in seconds})
        return weight_gradients(c, ring, SECOND, place, shared)[0], shared[N.grad_mod]

    def sums_of(grad_mod):
        given = jnp.sum(grad_mod[:, 0], axis=0, keepdims=True)
        return jnp.concatenate([given, grad_mod[:, 1]]).astype(bf16)

    if ring:
        *totals, sums = ring_sums(first, second, dp_index // 4, sums_of)
    else:
        group1, sums = second(())
        sums = gather_small(sums_of(sums))
        groups = first[0], group1, first[1]
        joined = [parts[0] for parts in groups]
        if not direct:
            tall = ratio * c.own
            joined = [
                jnp.concatenate(
                    [
                        part[:, i * c.own : (i + 1) * c.own].reshape(group, own, width)
                        for i in range(part.shape[1] // c.own)
                    ],
                    axis=1,
                )
                for part in (joined[0][:, tall:], joined[1], joined[2])
            ]
            tall = groups[0][0][:, :tall].reshape(group, ratio * own, width)
            joined[0] = jnp.concatenate([tall, joined[0]], axis=1)
        total = lax.psum_scatter(
            jnp.concatenate(joined, axis=1), DP, scatter_dimension=0, tiled=False
        ).astype(f32)
        cuts = (ratio + 1) * own, (2 * ratio + 4 - LEAD) * own
        totals = jnp.split(total, cuts)
    tall, rest = ratio * own, (ratio - LEAD) * own
    down, proj = totals[0][:tall], totals[0][tall:]
    up, qkv = jnp.concatenate([totals[2], totals[1][:rest]]), totals[1][rest:]
    grad_qkv = from_blocks(qkv, own, width)
    grad_proj = proj
    grad_up = from_blocks(up, own, width)
    grad_down = down

    sums = sums.reshape(group * (1 + micro_count), 6 * width)
    grad_ada = lax.dot_general(embed, sums, TN, preferred_element_type=f32)

    out_shape = (1, micro_count, 1, frames, patches, width)
    return (
        acts.reshape(out_shape),
        shared[N.grad_in].reshape(out_shape),
        grad_ada[None],
        grad_qkv[None],
        grad_proj[None],
        grad_up[None],
        grad_down[None],
    )


def solution(mesh):
    placed = (
        P(None, DP, None, None, None),
        P(None, DP, None, None, None),
        P(None, DP, None, None),
        P(None, DP),
        P(SECTION, DP, None),
        P(SECTION, DP, None),
        P(SECTION, DP, None),
        P(SECTION, DP, None),
        P(SECTION, DP, None),
    )
    return jax.shard_map(
        local,
        mesh=mesh,
        in_specs=placed,
        out_specs=(
            P(SECTION, None, DP, None, None, None),
            P(SECTION, None, DP, None, None, None),
            P(SECTION, DP, None),
            P(SECTION, DP, None),
            P(SECTION, DP, None),
            P(SECTION, DP, None),
            P(SECTION, DP, None),
        ),
        check_vma=False,
    )
```

profile of v0, /device:TPU:0, one launch (start us, length us, event | category | flops | bytes accessed | tf_op | source)
XLA Modules:
  0.0 359.5 jit_solution(8985227462995433688)
XLA Ops:
  7.2 1.1 convert_bitcast_fusion.1
  8.7 0.9 copy-done.21
  9.6 4.1 %collective-permute-start = (s32[1,2]{1,0:T(1,128)S(1)}, s32[1,2]{1,0:T(1,128)S(1)}, u32[]{:S(2)}, u32[]{:S(2)}) collective-permute-start(s32[1,2]{1,0:T(1,128)S(1)} %bitcast.147), channel_id=1, source_target_pairs={{0,8},{1,9},{2,10},{3,11},{4,12},{5,13},{6,14},{7,15},{8,0},{9,1},... | collective-permute-start | bytes 32 | tf_op jit(solution)/shard_map/ppermute | solution.py:958
  13.7 1.5 collective-permute-done
  15.2 2.0 collective-permute-start.1
  17.2 1.7 collective-permute-done.1
  19.1 1.8 collective-permute-start.2
  20.9 1.7 collective-permute-done.2
  22.8 1.1 collective-permute-done.3
  25.7 1.6 collective-permute-done.4
  28.1 1.9 collective-permute-start.5
  30.2 8.6 %collective-permute-done.5 = f32[4,3,4608]{2,0,1:T(4,128)S(1)} collective-permute-done((f32[4,3,4608]{2,0,1:T(4,128)S(1)}, f32[4,3,4608]{2,0,1:T(4,128)S(1)}, u32[]{:S(2)}, u32[]{:S(2)}) %collective-permute-start.5) | collective-permute-done | bytes 221216 | tf_op jit(solution)/shard_map/ppermute | solution.py:958
  39.9 1.6 collective-permute-start.6
  41.5 12.0 %collective-permute-done.6 = f32[2,3,4608]{2,0,1:T(2,128)S(1)} collective-permute-done((f32[2,3,4608]{2,0,1:T(2,128)S(1)}, f32[2,3,4608]{2,0,1:T(2,128)S(1)}, u32[]{:S(2)}, u32[]{:S(2)}) %collective-permute-start.6) | collective-permute-done | bytes 110624 | tf_op jit(solution)/shard_map/ppermute | solution.py:958
  54.3 5.3 %collective-permute-done.7 = f32[1,3,4608]{2,0,1:T(1,128)S(1)} collective-permute-done((f32[1,3,4608]{2,0,1:T(1,128)S(1)}, f32[1,3,4608]{2,0,1:T(1,128)S(1)}, u32[]{:S(2)}, u32[]{:S(2)}) %collective-permute-start.7) | collective-permute-done | bytes 55328 | tf_op jit(solution)/shard_map/ppermute | solution.py:958
  59.9 67.7 %all-gather.3.cloned.1.call-done = bf16[9216,768]{1,0:T(8,128)(2,1)} async-done(((bf16[576,768]{1,0:T(8,128)(2,1)}), bf16[9216,768]{1,0:T(8,128)(2,1)}) %all-gather.3.cloned.1.call-update) | async-done | bytes 14155792 | tf_op jit(solution)/shard_map/all_gather | solution.py:1037
  127.6 13.7 %shard_map.144 = (bf16[256,768]{1,0:T(8,128)(2,1)S(1)}, bf16[256,2304]{1,0:T(8,128)(2,1)}, bf16[256,768]{1,0:T(8,128)(2,1)}, f32[256,768]{1,0:T(8,128)}, f32[256...) custom-call(s32[9]{0:T(128)S(1)} %pad_add_fusion.4.refs_0_, ...), custom_call_target="tpu_custom_call" | custom-call | flops 3623878656 | bytes 20000000 | tf_op jit(solution)/shard_map/pallas_call | solution.py:742
  141.3 1.3 collective-permute-start.9
  142.8 12.7 %shard_map.145 = (f32[2,256,768]{2,1,0:T(8,128)}, bf16[256,768]{1,0:T(8,128)(2,1)S(1)}, bf16[256,2304]{1,0:T(8,128)(2,1)}, bf16[256,768]{1,0:T(8,128)(2,1)}, f32...) custom-call(s32[9]{0:T(128)S(1)} %pad_add_fusion.3.refs_0_, ...), custom_call_target="tpu_custom_call", output_to_operand_aliasing={{0}: (4, {})} | custom-call | flops 3623878656 | bytes 20000000 | tf_op jit(solution)/shard_map/pallas_call | solution.py:742
  155.5 1.3 collective-permute-start.8
  156.8 1.0 shard_map.146
  157.9 1.3 collective-permute-start.11
  159.2 6.7 %collective-permute-done.8.refs_1_ = bf16[256,768]{1,0:T(8,128)(2,1)S(1)} collective-permute-done((bf16[256,768]{1,0:T(8,128)(2,1)S(1)}, bf16[256,768]{1,0:T(8,128)(2,1)S(1)}, u32[]{:S(2)}, u32[]{:S(2)}) %collective-permute-start.8) | collective-permute-done | bytes 393248 | tf_op jit(solution)/shard_map/ppermute | solution.py:1096
  165.9 1.1 shard_map.147
  166.9 1.6 collective-permute-start.10
  168.5 13.7 %collective-permute-done.11.refs_3_ = bf16[256,768]{1,0:T(8,128)(2,1)S(1)} collective-permute-done((bf16[256,768]{1,0:T(8,128)(2,1)S(1)}, bf16[256,768]{1,0:T(8,128)(2,1)S(1)}, u32[]{:S(2)}, u32[]{:S(2)}) %collective-permute-start.11) | collective-permute-done | bytes 393248 | tf_op jit(solution)/shard_map/ppermute | solution.py:1118
  182.3 17.1 %shard_map.148 = (f32[2,256,768]{2,1,0:T(8,128)}, f32[2,2,4608]{2,1,0:T(2,128)}, bf16[512,768]{1,0:T(8,128)(2,1)}, bf16[512,2304]{1,0:T(8,128)(2,1)}, bf16[512,7...) custom-call(s32[9]{0:T(128)S(1)} %pad_add_fusion.4.refs_0_, ...), custom_call_target="tpu_custom_call", output_to_operand_aliasing={{0}: (11, {}), {1}: (12, {}), {2}: (13, {}), {3}: (14, {}),... | custom-call | flops 7247757312 | bytes 20000000 | tf_op jit(solution)/shard_map/pallas_call | solution.py:742
  199.4 1.5 collective-permute-done.10.refs_3_
  201.0 8.9 %shard_map.149 = (f32[2,2,4608]{2,1,0:T(2,128)}, bf16[512,768]{1,0:T(8,128)(2,1)}, bf16[512,3072]{1,0:T(8,128)(2,1)}, bf16[512,3072]{1,0:T(8,128)(2,1)}, bf16[51...) custom-call(s32[9]{0:T(128)S(1)} %pad_add_fusion.3.refs_0_, ...), custom_call_target="tpu_custom_call", output_to_operand_aliasing={{0}: (9, {}), {1}: (10, {}), {2}: (11, {}), {3}: (12, {}), ... | custom-call | flops 4831838208 | bytes 20000000 | tf_op jit(solution)/shard_map/pallas_call | solution.py:742
  209.8 9.7 %shard_map.150 = (bf16[4,240,768]{2,1,0:T(8,128)(2,1)}, bf16[4,240,768]{2,1,0:T(8,128)(2,1)S(1)}, bf16[4,240,768]{2,1,0:T(8,128)(2,1)}, bf16[4,240,768]{2,1,0:T(...) custom-call(s32[2]{0:T(128)S(1)} %pad_add_fusion.5.place, ...), custom_call_target="tpu_custom_call" | custom-call | flops 4227858432 | bytes 12000000 | tf_op jit(solution)/shard_map/pallas_call | solution.py:890
  220.1 4.8 %collective-permute-done.13 = bf16[4,2,96,768]{3,2,1,0:T(8,128)(2,1)} collective-permute-done((bf16[4,2,96,768]{3,2,1,0:T(8,128)(2,1)}, bf16[4,2,96,768]{3,2,1,0:T(8,128)(2,1)}, u32[]{:S(2)}, u32[]{:S(2)}) %collective-permute-start.13) | collective-permute-done | bytes 1179680 | tf_op jit(solution)/shard_map/ppermute | solution.py:958
  224.8 1.6 fusion.16
  226.5 1.9 add_convert_fusion.1
  229.0 1.3 collective-permute-start.15
  230.5 2.8 collective-permute-start.17
  233.4 5.0 %copy-done.1 = bf16[16,576,768]{2,1,0:T(8,128)(2,1)S(1)} copy-done((bf16[16,576,768]{2,1,0:T(8,128)(2,1)S(1)}, bf16[16,576,768]{2,1,0:T(8,128)(2,1)}, u32[]{:S(2)}) %copy-start.1) | copy-done | bytes 14155800
  238.4 10.5 %shard_map.151 = (f32[2,256,768]{2,1,0:T(8,128)}, f32[2,2,4608]{2,1,0:T(2,128)}, bf16[512,2304]{1,0:T(8,128)(2,1)}, bf16[512,768]{1,0:T(8,128)(2,1)}) custom-call(s32[9]{0:T(128)S(1)} %pad_add_fusion.3.refs_0_, f32[2,2,4608]{2,1,0:T(2,128)S(1)} %pad_maximum_fusion.3.refs_2_.refs_1_, ...), custom_call_target="tpu_custom_call", output_to_operand_aliasing={{0}: (7, {}), {1}: (8, {}), {2}: (9, {}), {3}: (10, {})} | custom-call | flops 2415919104 | bytes 20000000 | tf_op jit(solution)/shard_map/pallas_call | solution.py:742
  249.0 7.4 %shard_map.152 = (bf16[4,240,768]{2,1,0:T(8,128)(2,1)S(1)}, bf16[4,240,768]{2,1,0:T(8,128)(2,1)S(1)}, bf16[4,240,768]{2,1,0:T(8,128)(2,1)S(1)}, bf16[4,240,768]{2,1,0:T(8,128)(2,1)S(1)}) custom-call(s32[2]{0:T(128)S(1)} %pad_add_fusion.5.place, bf16[512,768]{1,0:T(8,128)(2,1)} %get-tuple-element.163.refs_2_.refs_0_, ...), custom_call_target="tpu_custom_call" | custom-call | flops 3019898880 | bytes 12000000 | tf_op jit(solution)/shard_map/pallas_call | solution.py:890
  257.1 5.6 %collective-permute-done.14 = bf16[4,240,768]{2,1,0:T(8,128)(2,1)S(1)} collective-permute-done((bf16[4,240,768]{2,1,0:T(8,128)(2,1)S(1)}, bf16[4,240,768]{2,1,0:T(8,128)(2,1)S(1)}, u32[]{:S(2)}, u32[]{:S(2)}) %collective-permute-start.14) | collective-permute-done | bytes 1474592 | tf_op jit(solution)/shard_map/ppermute | solution.py:958
  263.0 0.9 fusion.17
  264.6 1.5 collective-permute-done.19
  266.1 1.5 add_convert_fusion
  267.8 1.6 collective-permute-start.25
  270.2 2.5 collective-permute-done.25
  272.9 3.6 %fusion.8 = (bf16[240,768]{1,0:T(8,128)(2,1)}, bf16[240,768]{1,0:T(8,128)(2,1)}, bf16[240,768]{1,0:T(8,128)(2,1)}, bf16[240,768]{1,0:T(8,128)(2,1)S(1)}) fusion(bf16[4,240,768]{2,1,0:T(8,128)(2,1)} %copy-done.18, s32[]{:T(128)S(6)} %select_n.259, bf16[4,240,768]{2,1,0:T(8,128)(2,1)} %copy-done.19, bf16[4,240,768]{2,1,0:T(8,128)(2,1)} %get-tuple-element.185, ...), kind=kLoop, calls=%fused_computation.31 | loop fusion | flops 4423680 | bytes 5898256 | tf_op jit(solution)/shard_map/convert_element_type | solution.py:921
  276.5 2.9 collective-permute-start.20
  281.6 0.9 collective-permute-start.22
  282.5 1.0 convert_add_fusion.3
  284.2 6.1 %collective-permute-done.20 = bf16[240,768]{1,0:T(8,128)(2,1)} collective-permute-done((bf16[240,768]{1,0:T(8,128)(2,1)}, bf16[240,768]{1,0:T(8,128)(2,1)}, u32[]{:S(2)}, u32[]{:S(2)}) %collective-permute-start.20) | collective-permute-done | bytes 368672 | tf_op jit(solution)/shard_map/ppermute | solution.py:958
  290.3 21.3 %collective-permute-done.21 = bf16[240,768]{1,0:T(8,128)(2,1)} collective-permute-done((bf16[240,768]{1,0:T(8,128)(2,1)}, bf16[240,768]{1,0:T(8,128)(2,1)}, u32[]{:S(2)}, u32[]{:S(2)}) %collective-permute-start.21) | collective-permute-done | bytes 368672 | tf_op jit(solution)/shard_map/ppermute | solution.py:958
  311.6 1.5 collective-permute-done.23
  313.1 2.9 fusion.10
  315.9 1.2 collective-permute-start.29
  317.1 1.5 collective-permute-start.30
  318.6 1.7 collective-permute-start.31
  320.9 1.3 convert_add_fusion.1
  322.2 0.9 slice_bitcast_fusion
  323.0 2.1 collective-permute-done.27
  326.4 0.8 collective-permute-done.28
  327.9 1.4 convolution_bitcast_fusion
  329.6 19.3 %collective-permute-done.30 = bf16[240,768]{1,0:T(8,128)(2,1)} collective-permute-done((bf16[240,768]{1,0:T(8,128)(2,1)}, bf16[240,768]{1,0:T(8,128)(2,1)}, u32[]{:S(2)}, u32[]{:S(2)}) %collective-permute-start.30) | collective-permute-done | bytes 368672 | tf_op jit(solution)/shard_map/ppermute | solution.py:958
  349.0 1.7 fusion.1
  350.7 0.8 maximum_bitcast_fusion.1
  351.6 0.9 maximum_bitcast_fusion
  (167 shorter events, 15.7 us)
Async XLA Ops:
  7.2 1.3 copy-start.24
  7.2 1.3 copy-start.27
  7.2 1.4 copy-start.25
  7.2 120.4 %all-gather.3.cloned.1.call-start = ((), (), s32[]{:S(2)}) async-start(), calls=%async_computation | async-start | bytes 15040512 | tf_op jit(solution)/shard_map/all_gather | solution.py:1037
  8.5 1.1 copy-start.29
  8.5 15.7 %copy-start.22 = (f32[1,48,4608]{2,1,0:T(8,128)S(1)}, f32[1,48,4608]{2,1,0:T(8,128)}, u32[]{:S(2)}) copy-start(f32[1,48,4608]{2,1,0:T(8,128)} %param.13) | copy-start | bytes 2654212
  8.6 0.9 copy-start.21
  9.6 5.6 %collective-permute-start = (s32[1,2]{1,0:T(1,128)S(1)}, s32[1,2]{1,0:T(1,128)S(1)}, u32[]{:S(2)}, u32[]{:S(2)}) collective-permute-start(s32[1,2]{1,0:T(1,128)S(1)} %bitcast.147), channel_id=1, source_target_pairs={{0,8},{1,9},{2,10},{3,11},{4,12},{5,13},{6,14},{7,15},{8,0},{9,1},... | collective-permute-start | bytes 32 | tf_op jit(solution)/shard_map/ppermute | solution.py:958
  15.2 3.6 %collective-permute-start.1 = (s32[2,2]{1,0:T(2,128)S(1)}, s32[2,2]{1,0:T(2,128)S(1)}, u32[]{:S(2)}, u32[]{:S(2)}) collective-permute-start(s32[2,2]{1,0:T(2,128)S(1)} %add_bitcast_fusion), channel_id=1, source_target_pairs={{0,4},{1,5},{2,6},{3,7},{4,0},{5,1},{6,2},{7,3},{8,12},{9,13},{10,... | collective-permute-start | bytes 56 | tf_op jit(solution)/shard_map/ppermute | solution.py:958
  19.1 3.6 collective-permute-start.2
  22.8 1.1 collective-permute-start.3
  25.4 1.9 collective-permute-start.4
  25.7 4.3 %copy-start.28 = (s32[2,1,2,4]{3,2,1,0:T(2,128)S(1)}, s32[2,1,2,4]{3,2,1,0:T(2,128)}, u32[]{:S(2)}) copy-start(s32[2,1,2,4]{3,2,1,0:T(2,128)} %param.11) | copy-start | bytes 196
  28.1 10.7 %collective-permute-start.5 = (f32[4,3,4608]{2,0,1:T(4,128)S(1)}, f32[4,3,4608]{2,0,1:T(4,128)S(1)}, u32[]{:S(2)}, u32[]{:S(2)}) collective-permute-start(f32[4,3,4608]{2,0,1:T(4,128)S(1)} %broadcast_select_fusion.1), channel_id=1, source_target_pairs={{0,2},{1,3},{2,0},{3,1},{4,6},{5,7},{6,4},{7,5},{8,10},{9,11},{10,... | collective-permute-start | bytes 663560 | tf_op jit(solution)/shard_map/ppermute | solution.py:958
  30.1 97.5 %copy-start.2 = (bf16[2,1,2,128,768]{4,3,2,1,0:T(8,128)(2,1)S(1)}, bf16[2,1,2,128,768]{4,3,2,1,0:T(8,128)(2,1)}, u32[]{:S(2)}) copy-start(bf16[2,1,2,128,768]{4,3,2,1,0:T(8,128)(2,1)} %param.9) | copy-start | bytes 2359300
  39.9 13.6 %collective-permute-start.6 = (f32[2,3,4608]{2,0,1:T(2,128)S(1)}, f32[2,3,4608]{2,0,1:T(2,128)S(1)}, u32[]{:S(2)}, u32[]{:S(2)}) collective-permute-start(f32[2,3,4608]{2,0,1:T(2,128)S(1)} %broadcast_select_fusion.2), channel_id=1, source_target_pairs={{0,4},{1,5},{2,6},{3,7},{4,0},{5,1},{6,2},{7,3},{8,12},{9,13},{10,... | collective-permute-start | bytes 331784 | tf_op jit(solution)/shard_map/ppermute | solution.py:958
  53.7 6.0 %collective-permute-start.7 = (f32[1,3,4608]{2,0,1:T(1,128)S(1)}, f32[1,3,4608]{2,0,1:T(1,128)S(1)}, u32[]{:S(2)}, u32[]{:S(2)}) collective-permute-start(f32[1,3,4608]{2,0,1:T(1,128)S(1)} %broadcast_select_fusion.3), channel_id=1, source_target_pairs={{0,8},{1,9},{2,10},{3,11},{4,12},{5,13},{6,14},{7,15},{8,0},{9,1},... | collective-permute-start | bytes 165896 | tf_op jit(solution)/shard_map/ppermute | solution.py:958
  141.3 59.6 %copy-start = (bf16[16,576,768]{2,1,0:T(8,128)(2,1)}, bf16[16,576,768]{2,1,0:T(8,128)(2,1)S(1)}, u32[]{:S(2)}) copy-start(bf16[16,576,768]{2,1,0:T(8,128)(2,1)S(1)} %get-tuple-element.112.refs_3_.refs_2_) | copy-start | bytes 42467332
  141.3 15.5 %collective-permute-start.9 = (bf16[256,768]{1,0:T(8,128)(2,1)S(1)}, bf16[256,768]{1,0:T(8,128)(2,1)S(1)}, u32[]{:S(2)}, u32[]{:S(2)}) collective-permute-start(bf16[256,768]{1,0:T(8,128)(2,1)S(1)} %get-tuple-element.115), channel_id=1, source_target_pairs={{0,16},{1,17},{2,18},{3,19},{4,20},{5,21},{6,22},{7,23},{8,24},{9,... | collective-permute-start | bytes 1179656 | tf_op jit(solution)/shard_map/ppermute | solution.py:1096
  142.7 14.1 %copy-start.17 = (bf16[2,1,2,128,768]{4,3,2,1,0:T(8,128)(2,1)S(1)}, bf16[2,1,2,128,768]{4,3,2,1,0:T(8,128)(2,1)}, u32[]{:S(2)}) copy-start(bf16[2,1,2,128,768]{4,3,2,1,0:T(8,128)(2,1)} %param.10) | copy-start | bytes 2359300
  155.5 10.4 %collective-permute-start.8 = (bf16[256,768]{1,0:T(8,128)(2,1)S(1)}, bf16[256,768]{1,0:T(8,128)(2,1)S(1)}, u32[]{:S(2)}, u32[]{:S(2)}) collective-permute-start(bf16[256,768]{1,0:T(8,128)(2,1)S(1)} %get-tuple-element.114), channel_id=1, source_target_pairs={{0,16},{1,17},{2,18},{3,19},{4,20},{5,21},{6,22},{7,23},{8,24},{9,... | collective-permute-start | bytes 1179656 | tf_op jit(solution)/shard_map/ppermute | solution.py:1096
  157.9 24.4 %collective-permute-start.11 = (bf16[256,768]{1,0:T(8,128)(2,1)S(1)}, bf16[256,768]{1,0:T(8,128)(2,1)S(1)}, u32[]{:S(2)}, u32[]{:S(2)}) collective-permute-start(bf16[256,768]{1,0:T(8,128)(2,1)S(1)} %get-tuple-element.135), channel_id=1, source_target_pairs={{16,0},{17,1},{18,2},{19,3},{20,4},{21,5},{22,6},{23,7},{24,8},{25... | collective-permute-start | bytes 1179656 | tf_op jit(solution)/shard_map/ppermute | solution.py:1118
  165.9 16.4 %copy-start.3 = (f32[256,3072]{1,0:T(8,128)S(1)}, f32[256,3072]{1,0:T(8,128)}, u32[]{:S(2)}) copy-start(f32[256,3072]{1,0:T(8,128)} %get-tuple-element.140.refs_9_) | copy-start | bytes 9437188
  165.9 16.4 %copy-start.6 = (bf16[256,2304]{1,0:T(8,128)(2,1)S(1)}, bf16[256,2304]{1,0:T(8,128)(2,1)}, u32[]{:S(2)}) copy-start(bf16[256,2304]{1,0:T(8,128)(2,1)} %get-tuple-element.136.refs_5_) | copy-start | bytes 3538948
  165.9 16.4 %copy-start.8 = (f32[256,768]{1,0:T(8,128)S(1)}, f32[256,768]{1,0:T(8,128)}, u32[]{:S(2)}) copy-start(f32[256,768]{1,0:T(8,128)} %get-tuple-element.138.refs_7_) | copy-start | bytes 2359300
  165.9 16.4 %copy-start.9 = (f32[256,768]{1,0:T(8,128)S(1)}, f32[256,768]{1,0:T(8,128)}, u32[]{:S(2)}) copy-start(f32[256,768]{1,0:T(8,128)} %get-tuple-element.139.refs_8_) | copy-start | bytes 2359300
  165.9 16.4 %copy-start.10 = (f32[256,768]{1,0:T(8,128)S(1)}, f32[256,768]{1,0:T(8,128)}, u32[]{:S(2)}) copy-start(f32[256,768]{1,0:T(8,128)} %get-tuple-element.141.refs_10_) | copy-start | bytes 2359300
  165.9 16.4 %copy-start.14 = (bf16[256,768]{1,0:T(8,128)(2,1)S(1)}, bf16[256,768]{1,0:T(8,128)(2,1)}, u32[]{:S(2)}) copy-start(bf16[256,768]{1,0:T(8,128)(2,1)} %get-tuple-element.137.refs_6_) | copy-start | bytes 1179652
  166.9 34.0 %collective-permute-start.10 = (bf16[256,768]{1,0:T(8,128)(2,1)S(1)}, bf16[256,768]{1,0:T(8,128)(2,1)S(1)}, u32[]{:S(2)}, u32[]{:S(2)}) collective-permute-start(bf16[256,768]{1,0:T(8,128)(2,1)S(1)} %get-tuple-element.129), channel_id=1, source_target_pairs={{16,0},{17,1},{18,2},{19,3},{20,4},{21,5},{22,6},{23,7},{24,8},{25... | collective-permute-start | bytes 1179656 | tf_op jit(solution)/shard_map/ppermute | solution.py:1118
  182.3 18.7 %copy-start.4 = (f32[256,3072]{1,0:T(8,128)S(1)}, f32[256,3072]{1,0:T(8,128)}, u32[]{:S(2)}) copy-start(f32[256,3072]{1,0:T(8,128)} %get-tuple-element.131.refs_5_) | copy-start | bytes 9437188
  182.3 18.6 %copy-start.11 = (f32[256,768]{1,0:T(8,128)S(1)}, f32[256,768]{1,0:T(8,128)}, u32[]{:S(2)}) copy-start(f32[256,768]{1,0:T(8,128)} %get-tuple-element.133.refs_7_) | copy-start | bytes 2359300
  182.3 18.6 %copy-start.12 = (f32[256,768]{1,0:T(8,128)S(1)}, f32[256,768]{1,0:T(8,128)}, u32[]{:S(2)}) copy-start(f32[256,768]{1,0:T(8,128)} %get-tuple-element.132.refs_6_) | copy-start | bytes 2359300
  182.3 18.6 %copy-start.13 = (f32[256,768]{1,0:T(8,128)S(1)}, f32[256,768]{1,0:T(8,128)}, u32[]{:S(2)}) copy-start(f32[256,768]{1,0:T(8,128)} %get-tuple-element.130.refs_4_) | copy-start | bytes 2359300
  182.3 18.6 %copy-start.16 = (bf16[256,768]{1,0:T(8,128)(2,1)S(1)}, bf16[256,768]{1,0:T(8,128)(2,1)}, u32[]{:S(2)}) copy-start(bf16[256,768]{1,0:T(8,128)(2,1)} %get-tuple-element.134.refs_8_) | copy-start | bytes 1179652
  219.5 6.9 %collective-permute-start.12 = (bf16[4,240,768]{2,1,0:T(8,128)(2,1)}, bf16[4,240,768]{2,1,0:T(8,128)(2,1)}, u32[]{:S(2)}, u32[]{:S(2)}) collective-permute-start(bf16[4,240,768]{2,1,0:T(8,128)(2,1)} %get-tuple-element.168), channel_id=1, source_target_pairs={{0,1},{1,0},{2,3},{3,2},{4,5},{5,4},{6,7},{7,6},{8,9},{9,8},{10,11... | collective-permute-start | bytes 4423688 | tf_op jit(solution)/shard_map/ppermute | solution.py:958
  219.6 5.3 %collective-permute-start.13 = (bf16[4,2,96,768]{3,2,1,0:T(8,128)(2,1)}, bf16[4,2,96,768]{3,2,1,0:T(8,128)(2,1)}, u32[]{:S(2)}, u32[]{:S(2)}) collective-permute-start(bf16[4,2,96,768]{3,2,1,0:T(8,128)(2,1)} %get-tuple-element.170), channel_id=1, source_target_pairs={{0,1},{1,0},{2,3},{3,2},{4,5},{5,4},{6,7},{7,6},{8,9},{9,8},{10,11... | collective-permute-start | bytes 3538952 | tf_op jit(solution)/shard_map/ppermute | solution.py:958
  226.4 2.6 copy-start.30
  226.4 6.9 %copy-start.5 = (bf16[256,2304]{1,0:T(8,128)(2,1)S(1)}, bf16[256,2304]{1,0:T(8,128)(2,1)}, u32[]{:S(2)}) copy-start(bf16[256,2304]{1,0:T(8,128)(2,1)} %get-tuple-element.179.refs_6_) | copy-start | bytes 3538948
  226.4 6.9 %copy-start.7 = (f32[256,768]{1,0:T(8,128)S(1)}, f32[256,768]{1,0:T(8,128)}, u32[]{:S(2)}) copy-start(f32[256,768]{1,0:T(8,128)} %get-tuple-element.177.refs_4_) | copy-start | bytes 2359300
  226.4 6.9 %copy-start.15 = (bf16[256,768]{1,0:T(8,128)(2,1)S(1)}, bf16[256,768]{1,0:T(8,128)(2,1)}, u32[]{:S(2)}) copy-start(bf16[256,768]{1,0:T(8,128)(2,1)} %get-tuple-element.178.refs_5_) | copy-start | bytes 1179652
  228.3 34.4 %collective-permute-start.14 = (bf16[4,240,768]{2,1,0:T(8,128)(2,1)S(1)}, bf16[4,240,768]{2,1,0:T(8,128)(2,1)S(1)}, u32[]{:S(2)}, u32[]{:S(2)}) collective-permute-start(bf16[4,240,768]{2,1,0:T(8,128)(2,1)S(1)} %add_convert_fusion.1), channel_id=1, source_target_pairs={{0,2},{1,3},{2,0},{3,1},{4,6},{5,7},{6,4},{7,5},{8,10},{9,11},{10,... | collective-permute-start | bytes 4423688 | tf_op jit(solution)/shard_map/ppermute | solution.py:958
  229.0 33.8 %collective-permute-start.18 = (bf16[4,240,768]{2,1,0:T(8,128)(2,1)S(1)}, bf16[4,240,768]{2,1,0:T(8,128)(2,1)S(1)}, u32[]{:S(2)}, u32[]{:S(2)}) collective-permute-start(bf16[4,240,768]{2,1,0:T(8,128)(2,1)S(1)} %copy-done.30), channel_id=1, source_target_pairs={{0,1},{1,0},{2,3},{3,2},{4,5},{5,4},{6,7},{7,6},{8,9},{9,8},{10,11... | collective-permute-start | bytes 4423688 | tf_op jit(solution)/shard_map/ppermute | solution.py:958
  229.0 27.3 %collective-permute-start.15 = (bf16[2,96,768]{2,1,0:T(8,128)(2,1)S(1)}, bf16[2,96,768]{2,1,0:T(8,128)(2,1)S(1)}, u32[]{:S(2)}, u32[]{:S(2)}) collective-permute-start(bf16[2,96,768]{2,1,0:T(8,128)(2,1)S(1)} %get-tuple-element.174), channel_id=1, source_target_pairs={{0,12},{1,13},{2,14},{3,15},{4,8},{5,9},{6,10},{7,11},{8,4},{9,5},... | collective-permute-start | bytes 884744 | tf_op jit(solution)/shard_map/ppermute | solution.py:958
  230.3 26.8 %collective-permute-start.16 = (bf16[2,96,768]{2,1,0:T(8,128)(2,1)S(1)}, bf16[2,96,768]{2,1,0:T(8,128)(2,1)S(1)}, u32[]{:S(2)}, u32[]{:S(2)}) collective-permute-start(bf16[2,96,768]{2,1,0:T(8,128)(2,1)S(1)} %get-tuple-element.175), channel_id=1, source_target_pairs={{0,8},{1,9},{2,10},{3,11},{4,12},{5,13},{6,14},{7,15},{8,0},{9,1},... | collective-permute-start | bytes 884744 | tf_op jit(solution)/shard_map/ppermute | solution.py:958
  230.5 26.6 %collective-permute-start.17 = (bf16[2,96,768]{2,1,0:T(8,128)(2,1)S(1)}, bf16[2,96,768]{2,1,0:T(8,128)(2,1)S(1)}, u32[]{:S(2)}, u32[]{:S(2)}) collective-permute-start(bf16[2,96,768]{2,1,0:T(8,128)(2,1)S(1)} %get-tuple-element.176), channel_id=1, source_target_pairs={{0,4},{1,5},{2,6},{3,7},{4,0},{5,1},{6,2},{7,3},{8,12},{9,13},{10,... | collective-permute-start | bytes 884744 | tf_op jit(solution)/shard_map/ppermute | solution.py:958
  233.4 5.0 %copy-start.1 = (bf16[16,576,768]{2,1,0:T(8,128)(2,1)S(1)}, bf16[16,576,768]{2,1,0:T(8,128)(2,1)}, u32[]{:S(2)}) copy-start(bf16[16,576,768]{2,1,0:T(8,128)(2,1)} %copy-done) | copy-start | bytes 42467332
  262.7 4.8 %copy-start.18 = (bf16[4,240,768]{2,1,0:T(8,128)(2,1)}, bf16[4,240,768]{2,1,0:T(8,128)(2,1)S(1)}, u32[]{:S(2)}) copy-start(bf16[4,240,768]{2,1,0:T(8,128)(2,1)S(1)} %collective-permute-done.14) | copy-start | bytes 4423684
  262.7 4.9 %copy-start.19 = (bf16[4,240,768]{2,1,0:T(8,128)(2,1)}, bf16[4,240,768]{2,1,0:T(8,128)(2,1)S(1)}, u32[]{:S(2)}) copy-start(bf16[4,240,768]{2,1,0:T(8,128)(2,1)S(1)} %collective-permute-done.18) | copy-start | bytes 4423684
  262.7 3.3 collective-permute-start.19
  264.6 3.0 copy-start.20
  267.8 4.9 %collective-permute-start.25 = (bf16[1,3,4608]{2,1,0:T(4,128)(2,1)S(1)}, bf16[1,3,4608]{2,1,0:T(4,128)(2,1)S(1)}, u32[]{:S(2)}, u32[]{:S(2)}) collective-permute-start(bf16[1,3,4608]{2,1,0:T(4,128)(2,1)S(1)} %pad_maximum_fusion.6), channel_id=1, source_target_pairs={{0,8},{1,9},{2,10},{3,11},{4,12},{5,13},{6,14},{7,15},{8,0},{9,1},... | collective-permute-start | bytes 82952 | tf_op jit(solution)/shard_map/ppermute | solution.py:958
  269.5 14.7 %collective-permute-start.24 = (bf16[4,240,768]{2,1,0:T(8,128)(2,1)S(1)}, bf16[4,240,768]{2,1,0:T(8,128)(2,1)}, u32[]{:S(2)}, u32[]{:S(2)}) collective-permute-start(bf16[4,240,768]{2,1,0:T(8,128)(2,1)S(1)} %get-tuple-element.205), channel_id=1, source_target_pairs={{0,1},{1,0},{2,3},{3,2},{4,5},{5,4},{6,7},{7,6},{8,9},{9,8},{10,11... | collective-permute-start | bytes 4423688 | tf_op jit(solution)/shard_map/ppermute | solution.py:958
  269.6 12.0 %collective-permute-start.32 = (bf16[96,768]{1,0:T(8,128)(2,1)}, bf16[96,768]{1,0:T(8,128)(2,1)}, u32[]{:S(2)}, u32[]{:S(2)}) collective-permute-start(bf16[96,768]{1,0:T(8,128)(2,1)} %fusion.17), channel_id=1, source_target_pairs={{0,2},{1,3},{2,0},{3,1},{4,6},{5,7},{6,4},{7,5},{8,10},{9,11},{10,... | collective-permute-start | bytes 442376 | tf_op jit(solution)/shard_map/ppermute | solution.py:958
  272.9 7.2 %collective-permute-start.26 = (bf16[2,3,4608]{2,1,0:T(4,128)(2,1)S(1)}, bf16[2,3,4608]{2,1,0:T(4,128)(2,1)S(1)}, u32[]{:S(2)}, u32[]{:S(2)}) collective-permute-start(bf16[2,3,4608]{2,1,0:T(4,128)(2,1)S(1)} %maximum_bitcast_fusion.2), channel_id=1, source_target_pairs={{0,4},{1,5},{2,6},{3,7},{4,0},{5,1},{6,2},{7,3},{8,12},{9,13},{10,... | collective-permute-start | bytes 165896 | tf_op jit(solution)/shard_map/ppermute | solution.py:958
  276.5 13.7 %collective-permute-start.20 = (bf16[240,768]{1,0:T(8,128)(2,1)}, bf16[240,768]{1,0:T(8,128)(2,1)}, u32[]{:S(2)}, u32[]{:S(2)}) collective-permute-start(bf16[240,768]{1,0:T(8,128)(2,1)} %get-tuple-element.243), channel_id=1, source_target_pairs={{0,12},{1,13},{2,14},{3,15},{4,8},{5,9},{6,10},{7,11},{8,4},{9,5},... | collective-permute-start | bytes 1105928 | tf_op jit(solution)/shard_map/ppermute | solution.py:958
  279.5 32.1 %collective-permute-start.21 = (bf16[240,768]{1,0:T(8,128)(2,1)}, bf16[240,768]{1,0:T(8,128)(2,1)}, u32[]{:S(2)}, u32[]{:S(2)}) collective-permute-start(bf16[240,768]{1,0:T(8,128)(2,1)} %get-tuple-element.242), channel_id=1, source_target_pairs={{0,8},{1,9},{2,10},{3,11},{4,12},{5,13},{6,14},{7,15},{8,0},{9,1},... | collective-permute-start | bytes 1105928 | tf_op jit(solution)/shard_map/ppermute | solution.py:958
  280.0 33.1 %collective-permute-start.23 = (bf16[4,240,768]{2,1,0:T(8,128)(2,1)}, bf16[4,240,768]{2,1,0:T(8,128)(2,1)}, u32[]{:S(2)}, u32[]{:S(2)}) collective-permute-start(bf16[4,240,768]{2,1,0:T(8,128)(2,1)} %add_convert_fusion), channel_id=1, source_target_pairs={{0,2},{1,3},{2,0},{3,1},{4,6},{5,7},{6,4},{7,5},{8,10},{9,11},{10,... | collective-permute-start | bytes 4423688 | tf_op jit(solution)/shard_map/ppermute | solution.py:958
  281.6 30.0 %collective-permute-start.22 = (bf16[240,768]{1,0:T(8,128)(2,1)}, bf16[240,768]{1,0:T(8,128)(2,1)S(1)}, u32[]{:S(2)}, u32[]{:S(2)}) collective-permute-start(bf16[240,768]{1,0:T(8,128)(2,1)} %get-tuple-element.241), channel_id=1, source_target_pairs={{0,4},{1,5},{2,6},{3,7},{4,0},{5,1},{6,2},{7,3},{8,12},{9,13},{10,... | collective-permute-start | bytes 1105928 | tf_op jit(solution)/shard_map/ppermute | solution.py:958
  313.1 7.3 %copy-start.26 = (bf16[4,3,4608]{2,0,1:T(4,128)(2,1)S(1)}, bf16[4,3,4608]{2,0,1:T(4,128)(2,1)}, u32[]{:S(2)}) copy-start(bf16[4,3,4608]{2,0,1:T(4,128)(2,1)} %reshape.214) | copy-start | bytes 331780
  315.9 13.7 %collective-permute-start.29 = (bf16[240,768]{1,0:T(8,128)(2,1)}, bf16[240,768]{1,0:T(8,128)(2,1)}, u32[]{:S(2)}, u32[]{:S(2)}) collective-permute-start(bf16[240,768]{1,0:T(8,128)(2,1)} %get-tuple-element.238), channel_id=1, source_target_pairs={{0,12},{1,13},{2,14},{3,15},{4,8},{5,9},{6,10},{7,11},{8,4},{9,5},... | collective-permute-start | bytes 1105928 | tf_op jit(solution)/shard_map/ppermute | solution.py:958
  317.1 31.8 %collective-permute-start.30 = (bf16[240,768]{1,0:T(8,128)(2,1)}, bf16[240,768]{1,0:T(8,128)(2,1)}, u32[]{:S(2)}, u32[]{:S(2)}) collective-permute-start(bf16[240,768]{1,0:T(8,128)(2,1)} %get-tuple-element.240), channel_id=1, source_target_pairs={{0,8},{1,9},{2,10},{3,11},{4,12},{5,13},{6,14},{7,15},{8,0},{9,1},... | collective-permute-start | bytes 1105928 | tf_op jit(solution)/shard_map/ppermute | solution.py:958
  318.6 30.4 %collective-permute-start.31 = (bf16[240,768]{1,0:T(8,128)(2,1)}, bf16[240,768]{1,0:T(8,128)(2,1)}, u32[]{:S(2)}, u32[]{:S(2)}) collective-permute-start(bf16[240,768]{1,0:T(8,128)(2,1)} %get-tuple-element.239), channel_id=1, source_target_pairs={{0,4},{1,5},{2,6},{3,7},{4,0},{5,1},{6,2},{7,3},{8,12},{9,13},{10,... | collective-permute-start | bytes 1105928 | tf_op jit(solution)/shard_map/ppermute | solution.py:958
  320.3 4.7 %collective-permute-start.27 = (bf16[4,3,4608]{2,0,1:T(4,128)(2,1)S(1)}, bf16[4,3,4608]{2,0,1:T(4,128)(2,1)S(1)}, u32[]{:S(2)}, u32[]{:S(2)}) collective-permute-start(bf16[4,3,4608]{2,0,1:T(4,128)(2,1)S(1)} %copy-done.26), channel_id=1, source_target_pairs={{0,2},{1,3},{2,0},{3,1},{4,6},{5,7},{6,4},{7,5},{8,10},{9,11},{10,... | collective-permute-start | bytes 331784 | tf_op jit(solution)/shard_map/ppermute | solution.py:958
  325.6 1.5 collective-permute-start.28
  (1 other events, 0.9 us)
Sparse Core Ops, SparseCore 0:
  10.9 116.6 all-gather.2
where the time goes:
time: 366 us; the launch traced here: 359 us
  waiting for transfers between devices  190 us (52%)
  Pallas kernels  82 us (22%)
  starting transfers between devices  35.6 us (10%)
  other arithmetic  20.1 us (5%)
  local copies, waits for them, and re-layouts  15 us (4%)
  between operations  15 us (4%)
    ppermute x29, waiting for transfers between devices, swap(): return lax.ppermute(block, DP, [(i, i ^ distance) for i in range(count)])  100 us
    all_gather x1, waiting for transfers between devices, local(): weights = lax.all_gather(shard, DP, axis=0, tiled=False)  67.7 us
    pallas_call x7, Pallas kernels, call(): pl.pallas_call(lambda *refs: kernel(c, micro, names, refs), out_shape=sha...  65 us
    ppermute x29, starting transfers between devices, swap(): return lax.ppermute(block, DP, [(i, i ^ distance) for i in range(count)])  30.1 us
    pallas_call x2, Pallas kernels, weight_gradients(): pl.pallas_call(partial(gradients_kernel, c, ring, order), out_shape=out,...  17 us
    ppermute x2, waiting for transfers between devices, local(): grads.append(in_vmem(lax.ppermute(got[N.send], SECTION, [(1, 0)])))  15.2 us
    convert_element_type x3, other arithmetic, line_terms(): add(*[at(part, k) for part in parts]).astype(bf16)  8.04 us
  transfers between devices with their start and end apart: 34, of which 24 were waited for; matrix products, arithmetic and copies ran while one was open for 5% of the time, Pallas kernels for 14%

commit v1 on v0

--- a/solution.py
+++ b/solution.py
@@ -937,12 +937,12 @@
     core0 = swap(near_core0, 1)
 
     far0, terms2, core0, (near1, far1, *core1), small = meet((far0, terms2, core0, group1, small))
-    far1 = add(far1, swap(core1[1], 1)).astype(bf16)
+    far_core1 = swap(core1[1], 1)
     sum2 = add(*terms2)
     other2, sum2 = sum2[1].astype(bf16), sum2[0]
-    far0, far1, other2, sum2, small = meet((far0, far1, other2, sum2, small))
+    far0, far_core1, other2, sum2, small = meet((far0, far_core1, other2, sum2, small))
     terms0 = line_swap(line_terms(z, near0, core0, far0))
-    far1 = swap(far1, 2)
+    far1 = swap(add(far1, far_core1).astype(bf16), 2)
     core1 = swap(core1[0], 1)
     small = gather_step(gather_step(sums(small)[None], 8), 4)
 

time: 366 us -> 364 us (level)
  waiting for transfers between devices: 190 us -> 181 us
    ppermute x29, waiting for transfers between devices: 100 us -> 91.8 us  [swap(): return lax.ppermute(block, DP, [(i, i ^ distance) for i in range(count)])]
    unnamed x70 -> x80, local copies, waits for them, and re-layouts: 6.18 us -> 7.34 us
  transfers between devices with their start and end apart: 34 -> 34, of which waited for: 24 -> 21; matrix products, arithmetic and copies ran while one was open for 5% -> 7% of each run, Pallas kernels for 14% -> 14%
where the time goes in v1:
time: 364 us; the launch traced here: 357 us
  waiting for transfers between devices  181 us (50%)
  Pallas kernels  82.5 us (23%)
  starting transfers between devices  37.5 us (10%)
  other arithmetic  23.2 us (6%)
  local copies, waits for them, and re-layouts  15.9 us (4%)
  between operations  15 us (4%)
    ppermute x29, waiting for transfers between devices, swap(): return lax.ppermute(block, DP, [(i, i ^ distance) for i in range(count)])  91.8 us
    all_gather x1, waiting for transfers between devices, local(): weights = lax.all_gather(shard, DP, axis=0, tiled=False)  67.7 us
    pallas_call x7, Pallas kernels, call(): pl.pallas_call(lambda *refs: kernel(c, micro, names, refs), out_shape=sha...  65 us
    ppermute x29, starting transfers between devices, swap(): return lax.ppermute(block, DP, [(i, i ^ distance) for i in range(count)])  32 us
    pallas_call x2, Pallas kernels, weight_gradients(): pl.pallas_call(partial(gradients_kernel, c, ring, order), out_shape=out,...  17.5 us
    ppermute x2, waiting for transfers between devices, local(): grads.append(in_vmem(lax.ppermute(got[N.send], SECTION, [(1, 0)])))  15.2 us
    convert_element_type x3, other arithmetic, line_terms(): add(*[at(part, k) for part in parts]).astype(bf16)  8.55 us
    unnamed x80, local copies, waits for them, and re-layouts  7.34 us
  transfers between devices with their start and end apart: 34, of which 21 were waited for; matrix products, arithmetic and copies ran while one was open for 7% of the time, Pallas kernels for 14%

profile of v1, /device:TPU:0, one launch (start us, length us, event | category | flops | bytes accessed | tf_op | source)
XLA Modules:
  0.0 357.4 jit_solution(2349285464067757814)
XLA Ops:
  7.2 1.1 convert_bitcast_fusion.1
  8.7 0.9 copy-done.23
  9.6 4.1 %collective-permute-start = (s32[1,2]{1,0:T(1,128)S(1)}, s32[1,2]{1,0:T(1,128)S(1)}, u32[]{:S(2)}, u32[]{:S(2)}) collective-permute-start(s32[1,2]{1,0:T(1,128)S(1)} %bitcast.147), channel_id=1, source_target_pairs={{0,8},{1,9},{2,10},{3,11},{4,12},{5,13},{6,14},{7,15},{8,0},{9,1},... | collective-permute-start | bytes 32 | tf_op jit(solution)/shard_map/ppermute | solution.py:958
  13.7 1.5 collective-permute-done
  15.2 2.0 collective-permute-start.1
  17.2 1.7 collective-permute-done.1
  19.1 1.8 collective-permute-start.2
  20.9 1.7 collective-permute-done.2
  22.8 1.1 collective-permute-done.3
  25.7 1.6 collective-permute-done.4
  28.1 1.9 collective-permute-start.5
  30.2 8.6 %collective-permute-done.5 = f32[4,3,4608]{2,0,1:T(4,128)S(1)} collective-permute-done((f32[4,3,4608]{2,0,1:T(4,128)S(1)}, f32[4,3,4608]{2,0,1:T(4,128)S(1)}, u32[]{:S(2)}, u32[]{:S(2)}) %collective-permute-start.5) | collective-permute-done | bytes 221216 | tf_op jit(solution)/shard_map/ppermute | solution.py:958
  39.9 1.6 collective-permute-start.6
  41.5 12.0 %collective-permute-done.6 = f32[2,3,4608]{2,0,1:T(2,128)S(1)} collective-permute-done((f32[2,3,4608]{2,0,1:T(2,128)S(1)}, f32[2,3,4608]{2,0,1:T(2,128)S(1)}, u32[]{:S(2)}, u32[]{:S(2)}) %collective-permute-start.6) | collective-permute-done | bytes 110624 | tf_op jit(solution)/shard_map/ppermute | solution.py:958
  54.4 5.3 %collective-permute-done.7 = f32[1,3,4608]{2,0,1:T(1,128)S(1)} collective-permute-done((f32[1,3,4608]{2,0,1:T(1,128)S(1)}, f32[1,3,4608]{2,0,1:T(1,128)S(1)}, u32[]{:S(2)}, u32[]{:S(2)}) %collective-permute-start.7) | collective-permute-done | bytes 55328 | tf_op jit(solution)/shard_map/ppermute | solution.py:958
  59.9 67.7 %all-gather.3.cloned.1.call-done = bf16[9216,768]{1,0:T(8,128)(2,1)} async-done(((bf16[576,768]{1,0:T(8,128)(2,1)}), bf16[9216,768]{1,0:T(8,128)(2,1)}) %all-gather.3.cloned.1.call-update) | async-done | bytes 14155792 | tf_op jit(solution)/shard_map/all_gather | solution.py:1037
  127.6 13.7 %shard_map.144 = (bf16[256,768]{1,0:T(8,128)(2,1)S(1)}, bf16[256,2304]{1,0:T(8,128)(2,1)}, bf16[256,768]{1,0:T(8,128)(2,1)}, f32[256,768]{1,0:T(8,128)}, f32[256...) custom-call(s32[9]{0:T(128)S(1)} %pad_add_fusion.4.refs_0_, ...), custom_call_target="tpu_custom_call" | custom-call | flops 3623878656 | bytes 20000000 | tf_op jit(solution)/shard_map/pallas_call | solution.py:742
  141.3 1.3 collective-permute-start.9
  142.7 12.7 %shard_map.145 = (f32[2,256,768]{2,1,0:T(8,128)}, bf16[256,768]{1,0:T(8,128)(2,1)S(1)}, bf16[256,2304]{1,0:T(8,128)(2,1)}, bf16[256,768]{1,0:T(8,128)(2,1)}, f32...) custom-call(s32[9]{0:T(128)S(1)} %pad_add_fusion.3.refs_0_, ...), custom_call_target="tpu_custom_call", output_to_operand_aliasing={{0}: (4, {})} | custom-call | flops 3623878656 | bytes 20000000 | tf_op jit(solution)/shard_map/pallas_call | solution.py:742
  155.5 1.3 collective-permute-start.8
  156.8 1.0 shard_map.146
  157.8 1.3 collective-permute-start.11
  159.1 6.7 %collective-permute-done.8.refs_1_ = bf16[256,768]{1,0:T(8,128)(2,1)S(1)} collective-permute-done((bf16[256,768]{1,0:T(8,128)(2,1)S(1)}, bf16[256,768]{1,0:T(8,128)(2,1)S(1)}, u32[]{:S(2)}, u32[]{:S(2)}) %collective-permute-start.8) | collective-permute-done | bytes 393248 | tf_op jit(solution)/shard_map/ppermute | solution.py:1096
  165.9 1.1 shard_map.147
  166.9 1.6 collective-permute-start.10
  168.5 13.7 %collective-permute-done.11.refs_3_ = bf16[256,768]{1,0:T(8,128)(2,1)S(1)} collective-permute-done((bf16[256,768]{1,0:T(8,128)(2,1)S(1)}, bf16[256,768]{1,0:T(8,128)(2,1)S(1)}, u32[]{:S(2)}, u32[]{:S(2)}) %collective-permute-start.11) | collective-permute-done | bytes 393248 | tf_op jit(solution)/shard_map/ppermute | solution.py:1118
  182.3 17.1 %shard_map.148 = (f32[2,256,768]{2,1,0:T(8,128)}, f32[2,2,4608]{2,1,0:T(2,128)}, bf16[512,768]{1,0:T(8,128)(2,1)}, bf16[512,2304]{1,0:T(8,128)(2,1)}, bf16[512,7...) custom-call(s32[9]{0:T(128)S(1)} %pad_add_fusion.4.refs_0_, ...), custom_call_target="tpu_custom_call", output_to_operand_aliasing={{0}: (11, {}), {1}: (12, {}), {2}: (13, {}), {3}: (14, {}),... | custom-call | flops 7247757312 | bytes 20000000 | tf_op jit(solution)/shard_map/pallas_call | solution.py:742
  199.4 1.5 collective-permute-done.10.refs_3_
  200.9 8.9 %shard_map.149 = (f32[2,2,4608]{2,1,0:T(2,128)}, bf16[512,768]{1,0:T(8,128)(2,1)}, bf16[512,3072]{1,0:T(8,128)(2,1)}, bf16[512,3072]{1,0:T(8,128)(2,1)}, bf16[51...) custom-call(s32[9]{0:T(128)S(1)} %pad_add_fusion.3.refs_0_, ...), custom_call_target="tpu_custom_call", output_to_operand_aliasing={{0}: (9, {}), {1}: (10, {}), {2}: (11, {}), {3}: (12, {}), ... | custom-call | flops 4831838208 | bytes 20000000 | tf_op jit(solution)/shard_map/pallas_call | solution.py:742
  209.8 9.6 %shard_map.150 = (bf16[4,240,768]{2,1,0:T(8,128)(2,1)}, bf16[4,240,768]{2,1,0:T(8,128)(2,1)S(1)}, bf16[4,240,768]{2,1,0:T(8,128)(2,1)}, bf16[4,240,768]{2,1,0:T(...) custom-call(s32[2]{0:T(128)S(1)} %pad_add_fusion.5.place, ...), custom_call_target="tpu_custom_call" | custom-call | flops 4227858432 | bytes 12000000 | tf_op jit(solution)/shard_map/pallas_call | solution.py:890
  220.0 4.8 %collective-permute-done.13 = bf16[4,2,96,768]{3,2,1,0:T(8,128)(2,1)} collective-permute-done((bf16[4,2,96,768]{3,2,1,0:T(8,128)(2,1)}, bf16[4,2,96,768]{3,2,1,0:T(8,128)(2,1)}, u32[]{:S(2)}, u32[]{:S(2)}) %collective-permute-start.13) | collective-permute-done | bytes 1179680 | tf_op jit(solution)/shard_map/ppermute | solution.py:958
  224.8 2.3 fusion.16
  227.1 2.0 add_convert_fusion.1
  229.7 1.3 collective-permute-start.15
  231.2 2.8 collective-permute-start.17
  234.1 5.0 %copy-done.1 = bf16[16,576,768]{2,1,0:T(8,128)(2,1)S(1)} copy-done((bf16[16,576,768]{2,1,0:T(8,128)(2,1)S(1)}, bf16[16,576,768]{2,1,0:T(8,128)(2,1)}, u32[]{:S(2)}) %copy-start.1) | copy-done | bytes 14155800
  239.1 10.5 %shard_map.151 = (f32[2,256,768]{2,1,0:T(8,128)}, f32[2,2,4608]{2,1,0:T(2,128)}, bf16[512,2304]{1,0:T(8,128)(2,1)}, bf16[512,768]{1,0:T(8,128)(2,1)}) custom-call(s32[9]{0:T(128)S(1)} %pad_add_fusion.3.refs_0_, f32[2,2,4608]{2,1,0:T(2,128)S(1)} %pad_maximum_fusion.3.refs_2_.refs_1_, ...), custom_call_target="tpu_custom_call", output_to_operand_aliasing={{0}: (7, {}), {1}: (8, {}), {2}: (9, {}), {3}: (10, {})} | custom-call | flops 2415919104 | bytes 20000000 | tf_op jit(solution)/shard_map/pallas_call | solution.py:742
  249.7 7.9 %shard_map.152 = (bf16[4,240,768]{2,1,0:T(8,128)(2,1)S(1)}, bf16[4,240,768]{2,1,0:T(8,128)(2,1)S(1)}, bf16[4,240,768]{2,1,0:T(8,128)(2,1)S(1)}, bf16[4,240,768]{2,1,0:T(8,128)(2,1)}) custom-call(s32[2]{0:T(128)S(1)} %pad_add_fusion.5.place, bf16[512,768]{1,0:T(8,128)(2,1)} %get-tuple-element.163.refs_2_.refs_0_, ...), custom_call_target="tpu_custom_call" | custom-call | flops 3019898880 | bytes 12000000 | tf_op jit(solution)/shard_map/pallas_call | solution.py:890
  257.6 1.1 copy-done.17
  258.7 4.8 %collective-permute-done.14 = bf16[4,240,768]{2,1,0:T(8,128)(2,1)} collective-permute-done((bf16[4,240,768]{2,1,0:T(8,128)(2,1)S(1)}, bf16[4,240,768]{2,1,0:T(8,128)(2,1)}, u32[]{:S(2)}, u32[]{:S(2)}) %collective-permute-start.14) | collective-permute-done | bytes 1474592 | tf_op jit(solution)/shard_map/ppermute | solution.py:958
  264.4 1.3 convert_add_fusion.2
  266.3 0.7 slice_bitcast_fusion.1
  268.1 1.6 collective-permute-start.25
  269.6 2.9 add_convert_fusion
  272.5 1.5 collective-permute-start.23
  274.6 3.2 fusion.8
  277.8 2.4 collective-permute-start.20
  281.2 0.7 reshape.214
  281.9 1.3 collective-permute-start.22
  283.2 1.0 convert_add_fusion.3
  284.9 6.6 %collective-permute-done.20 = bf16[240,768]{1,0:T(8,128)(2,1)} collective-permute-done((bf16[240,768]{1,0:T(8,128)(2,1)}, bf16[240,768]{1,0:T(8,128)(2,1)}, u32[]{:S(2)}, u32[]{:S(2)}) %collective-permute-start.20) | collective-permute-done | bytes 368672 | tf_op jit(solution)/shard_map/ppermute | solution.py:958
  291.5 20.8 %collective-permute-done.21 = bf16[240,768]{1,0:T(8,128)(2,1)} collective-permute-done((bf16[240,768]{1,0:T(8,128)(2,1)}, bf16[240,768]{1,0:T(8,128)(2,1)}, u32[]{:S(2)}, u32[]{:S(2)}) %collective-permute-start.21) | collective-permute-done | bytes 368672 | tf_op jit(solution)/shard_map/ppermute | solution.py:958
  312.4 3.1 fusion.10
  315.5 1.2 collective-permute-start.29
  316.6 3.2 collective-permute-start.31
  320.4 1.3 convert_add_fusion.1
  321.7 0.9 slice_bitcast_fusion
  322.5 2.1 collective-permute-done.27
  325.9 0.8 collective-permute-done.28
  327.5 1.4 convolution_bitcast_fusion
  329.2 17.7 %collective-permute-done.30 = bf16[240,768]{1,0:T(8,128)(2,1)} collective-permute-done((bf16[240,768]{1,0:T(8,128)(2,1)}, bf16[240,768]{1,0:T(8,128)(2,1)}, u32[]{:S(2)}, u32[]{:S(2)}) %collective-permute-start.30) | collective-permute-done | bytes 368672 | tf_op jit(solution)/shard_map/ppermute | solution.py:958
  346.9 1.7 fusion.1
  348.7 0.8 maximum_bitcast_fusion.1
  349.6 0.9 maximum_bitcast_fusion
  (177 shorter events, 14.8 us)
Async XLA Ops:
  7.2 1.4 copy-start.27
  7.2 120.4 %all-gather.3.cloned.1.call-start = ((), (), s32[]{:S(2)}) async-start(), calls=%async_computation | async-start | bytes 15040512 | tf_op jit(solution)/shard_map/all_gather | solution.py:1037
  8.5 15.7 %copy-start.24 = (f32[1,48,4608]{2,1,0:T(8,128)S(1)}, f32[1,48,4608]{2,1,0:T(8,128)}, u32[]{:S(2)}) copy-start(f32[1,48,4608]{2,1,0:T(8,128)} %param.13) | copy-start | bytes 2654212
  9.6 5.6 %collective-permute-start = (s32[1,2]{1,0:T(1,128)S(1)}, s32[1,2]{1,0:T(1,128)S(1)}, u32[]{:S(2)}, u32[]{:S(2)}) collective-permute-start(s32[1,2]{1,0:T(1,128)S(1)} %bitcast.147), channel_id=1, source_target_pairs={{0,8},{1,9},{2,10},{3,11},{4,12},{5,13},{6,14},{7,15},{8,0},{9,1},... | collective-permute-start | bytes 32 | tf_op jit(solution)/shard_map/ppermute | solution.py:958
  15.2 3.6 %collective-permute-start.1 = (s32[2,2]{1,0:T(2,128)S(1)}, s32[2,2]{1,0:T(2,128)S(1)}, u32[]{:S(2)}, u32[]{:S(2)}) collective-permute-start(s32[2,2]{1,0:T(2,128)S(1)} %add_bitcast_fusion), channel_id=1, source_target_pairs={{0,4},{1,5},{2,6},{3,7},{4,0},{5,1},{6,2},{7,3},{8,12},{9,13},{10,... | collective-permute-start | bytes 56 | tf_op jit(solution)/shard_map/ppermute | solution.py:958
  19.1 3.6 collective-permute-start.2
  22.8 1.1 collective-permute-start.3
  25.4 1.9 collective-permute-start.4
  25.7 4.3 %copy-start.33 = (s32[2,1,2,4]{3,2,1,0:T(2,128)S(1)}, s32[2,1,2,4]{3,2,1,0:T(2,128)}, u32[]{:S(2)}) copy-start(s32[2,1,2,4]{3,2,1,0:T(2,128)} %param.11) | copy-start | bytes 196
  28.1 10.7 %collective-permute-start.5 = (f32[4,3,4608]{2,0,1:T(4,128)S(1)}, f32[4,3,4608]{2,0,1:T(4,128)S(1)}, u32[]{:S(2)}, u32[]{:S(2)}) collective-permute-start(f32[4,3,4608]{2,0,1:T(4,128)S(1)} %broadcast_select_fusion.1), channel_id=1, source_target_pairs={{0,2},{1,3},{2,0},{3,1},{4,6},{5,7},{6,4},{7,5},{8,10},{9,11},{10,... | collective-permute-start | bytes 663560 | tf_op jit(solution)/shard_map/ppermute | solution.py:958
  30.1 97.5 %copy-start.2 = (bf16[2,1,2,128,768]{4,3,2,1,0:T(8,128)(2,1)S(1)}, bf16[2,1,2,128,768]{4,3,2,1,0:T(8,128)(2,1)}, u32[]{:S(2)}) copy-start(bf16[2,1,2,128,768]{4,3,2,1,0:T(8,128)(2,1)} %param.9) | copy-start | bytes 2359300
  39.9 13.6 %collective-permute-start.6 = (f32[2,3,4608]{2,0,1:T(2,128)S(1)}, f32[2,3,4608]{2,0,1:T(2,128)S(1)}, u32[]{:S(2)}, u32[]{:S(2)}) collective-permute-start(f32[2,3,4608]{2,0,1:T(2,128)S(1)} %broadcast_select_fusion.2), channel_id=1, source_target_pairs={{0,4},{1,5},{2,6},{3,7},{4,0},{5,1},{6,2},{7,3},{8,12},{9,13},{10,... | collective-permute-start | bytes 331784 | tf_op jit(solution)/shard_map/ppermute | solution.py:958
  53.7 6.0 %collective-permute-start.7 = (f32[1,3,4608]{2,0,1:T(1,128)S(1)}, f32[1,3,4608]{2,0,1:T(1,128)S(1)}, u32[]{:S(2)}, u32[]{:S(2)}) collective-permute-start(f32[1,3,4608]{2,0,1:T(1,128)S(1)} %broadcast_select_fusion.3), channel_id=1, source_target_pairs={{0,8},{1,9},{2,10},{3,11},{4,12},{5,13},{6,14},{7,15},{8,0},{9,1},... | collective-permute-start | bytes 165896 | tf_op jit(solution)/shard_map/ppermute | solution.py:958
  141.3 59.6 %copy-start = (bf16[16,576,768]{2,1,0:T(8,128)(2,1)}, bf16[16,576,768]{2,1,0:T(8,128)(2,1)S(1)}, u32[]{:S(2)}) copy-start(bf16[16,576,768]{2,1,0:T(8,128)(2,1)S(1)} %get-tuple-element.112.refs_3_.refs_2_) | copy-start | bytes 42467332
  141.3 15.5 %collective-permute-start.9 = (bf16[256,768]{1,0:T(8,128)(2,1)S(1)}, bf16[256,768]{1,0:T(8,128)(2,1)S(1)}, u32[]{:S(2)}, u32[]{:S(2)}) collective-permute-start(bf16[256,768]{1,0:T(8,128)(2,1)S(1)} %get-tuple-element.115), channel_id=1, source_target_pairs={{0,16},{1,17},{2,18},{3,19},{4,20},{5,21},{6,22},{7,23},{8,24},{9,... | collective-permute-start | bytes 1179656 | tf_op jit(solution)/shard_map/ppermute | solution.py:1096
  142.7 14.1 %copy-start.18 = (bf16[2,1,2,128,768]{4,3,2,1,0:T(8,128)(2,1)S(1)}, bf16[2,1,2,128,768]{4,3,2,1,0:T(8,128)(2,1)}, u32[]{:S(2)}) copy-start(bf16[2,1,2,128,768]{4,3,2,1,0:T(8,128)(2,1)} %param.10) | copy-start | bytes 2359300
  155.5 10.4 %collective-permute-start.8 = (bf16[256,768]{1,0:T(8,128)(2,1)S(1)}, bf16[256,768]{1,0:T(8,128)(2,1)S(1)}, u32[]{:S(2)}, u32[]{:S(2)}) collective-permute-start(bf16[256,768]{1,0:T(8,128)(2,1)S(1)} %get-tuple-element.114), channel_id=1, source_target_pairs={{0,16},{1,17},{2,18},{3,19},{4,20},{5,21},{6,22},{7,23},{8,24},{9,... | collective-permute-start | bytes 1179656 | tf_op jit(solution)/shard_map/ppermute | solution.py:1096
  157.8 24.4 %collective-permute-start.11 = (bf16[256,768]{1,0:T(8,128)(2,1)S(1)}, bf16[256,768]{1,0:T(8,128)(2,1)S(1)}, u32[]{:S(2)}, u32[]{:S(2)}) collective-permute-start(bf16[256,768]{1,0:T(8,128)(2,1)S(1)} %get-tuple-element.135), channel_id=1, source_target_pairs={{16,0},{17,1},{18,2},{19,3},{20,4},{21,5},{22,6},{23,7},{24,8},{25... | collective-permute-start | bytes 1179656 | tf_op jit(solution)/shard_map/ppermute | solution.py:1118
  165.8 16.4 %copy-start.3 = (f32[256,3072]{1,0:T(8,128)S(1)}, f32[256,3072]{1,0:T(8,128)}, u32[]{:S(2)}) copy-start(f32[256,3072]{1,0:T(8,128)} %get-tuple-element.140.refs_9_) | copy-start | bytes 9437188
  165.8 16.4 %copy-start.6 = (bf16[256,2304]{1,0:T(8,128)(2,1)S(1)}, bf16[256,2304]{1,0:T(8,128)(2,1)}, u32[]{:S(2)}) copy-start(bf16[256,2304]{1,0:T(8,128)(2,1)} %get-tuple-element.136.refs_5_) | copy-start | bytes 3538948
  165.8 16.4 %copy-start.8 = (f32[256,768]{1,0:T(8,128)S(1)}, f32[256,768]{1,0:T(8,128)}, u32[]{:S(2)}) copy-start(f32[256,768]{1,0:T(8,128)} %get-tuple-element.138.refs_7_) | copy-start | bytes 2359300
  165.8 16.4 %copy-start.9 = (f32[256,768]{1,0:T(8,128)S(1)}, f32[256,768]{1,0:T(8,128)}, u32[]{:S(2)}) copy-start(f32[256,768]{1,0:T(8,128)} %get-tuple-element.139.refs_8_) | copy-start | bytes 2359300
  165.8 16.4 %copy-start.10 = (f32[256,768]{1,0:T(8,128)S(1)}, f32[256,768]{1,0:T(8,128)}, u32[]{:S(2)}) copy-start(f32[256,768]{1,0:T(8,128)} %get-tuple-element.141.refs_10_) | copy-start | bytes 2359300
  165.8 16.4 %copy-start.14 = (bf16[256,768]{1,0:T(8,128)(2,1)S(1)}, bf16[256,768]{1,0:T(8,128)(2,1)}, u32[]{:S(2)}) copy-start(bf16[256,768]{1,0:T(8,128)(2,1)} %get-tuple-element.137.refs_6_) | copy-start | bytes 1179652
  166.9 34.0 %collective-permute-start.10 = (bf16[256,768]{1,0:T(8,128)(2,1)S(1)}, bf16[256,768]{1,0:T(8,128)(2,1)S(1)}, u32[]{:S(2)}, u32[]{:S(2)}) collective-permute-start(bf16[256,768]{1,0:T(8,128)(2,1)S(1)} %get-tuple-element.129), channel_id=1, source_target_pairs={{16,0},{17,1},{18,2},{19,3},{20,4},{21,5},{22,6},{23,7},{24,8},{25... | collective-permute-start | bytes 1179656 | tf_op jit(solution)/shard_map/ppermute | solution.py:1118
  182.2 18.7 %copy-start.4 = (f32[256,3072]{1,0:T(8,128)S(1)}, f32[256,3072]{1,0:T(8,128)}, u32[]{:S(2)}) copy-start(f32[256,3072]{1,0:T(8,128)} %get-tuple-element.131.refs_5_) | copy-start | bytes 9437188
  182.3 18.6 %copy-start.11 = (f32[256,768]{1,0:T(8,128)S(1)}, f32[256,768]{1,0:T(8,128)}, u32[]{:S(2)}) copy-start(f32[256,768]{1,0:T(8,128)} %get-tuple-element.133.refs_7_) | copy-start | bytes 2359300
  182.3 18.6 %copy-start.12 = (f32[256,768]{1,0:T(8,128)S(1)}, f32[256,768]{1,0:T(8,128)}, u32[]{:S(2)}) copy-start(f32[256,768]{1,0:T(8,128)} %get-tuple-element.132.refs_6_) | copy-start | bytes 2359300
  182.3 18.6 %copy-start.13 = (f32[256,768]{1,0:T(8,128)S(1)}, f32[256,768]{1,0:T(8,128)}, u32[]{:S(2)}) copy-start(f32[256,768]{1,0:T(8,128)} %get-tuple-element.130.refs_4_) | copy-start | bytes 2359300
  182.3 18.6 %copy-start.16 = (bf16[256,768]{1,0:T(8,128)(2,1)S(1)}, bf16[256,768]{1,0:T(8,128)(2,1)}, u32[]{:S(2)}) copy-start(bf16[256,768]{1,0:T(8,128)(2,1)} %get-tuple-element.134.refs_8_) | copy-start | bytes 1179652
  219.4 7.6 %collective-permute-start.12 = (bf16[4,240,768]{2,1,0:T(8,128)(2,1)}, bf16[4,240,768]{2,1,0:T(8,128)(2,1)}, u32[]{:S(2)}, u32[]{:S(2)}) collective-permute-start(bf16[4,240,768]{2,1,0:T(8,128)(2,1)} %get-tuple-element.168), channel_id=1, source_target_pairs={{0,1},{1,0},{2,3},{3,2},{4,5},{5,4},{6,7},{7,6},{8,9},{9,8},{10,11... | collective-permute-start | bytes 4423688 | tf_op jit(solution)/shard_map/ppermute | solution.py:958
  219.5 5.3 %collective-permute-start.13 = (bf16[4,2,96,768]{3,2,1,0:T(8,128)(2,1)}, bf16[4,2,96,768]{3,2,1,0:T(8,128)(2,1)}, u32[]{:S(2)}, u32[]{:S(2)}) collective-permute-start(bf16[4,2,96,768]{3,2,1,0:T(8,128)(2,1)} %get-tuple-element.170), channel_id=1, source_target_pairs={{0,1},{1,0},{2,3},{3,2},{4,5},{5,4},{6,7},{7,6},{8,9},{9,8},{10,11... | collective-permute-start | bytes 3538952 | tf_op jit(solution)/shard_map/ppermute | solution.py:958
  227.1 2.6 copy-start.35
  227.1 7.0 %copy-start.5 = (bf16[256,2304]{1,0:T(8,128)(2,1)S(1)}, bf16[256,2304]{1,0:T(8,128)(2,1)}, u32[]{:S(2)}) copy-start(bf16[256,2304]{1,0:T(8,128)(2,1)} %get-tuple-element.179.refs_6_) | copy-start | bytes 3538948
  227.1 7.0 %copy-start.7 = (f32[256,768]{1,0:T(8,128)S(1)}, f32[256,768]{1,0:T(8,128)}, u32[]{:S(2)}) copy-start(f32[256,768]{1,0:T(8,128)} %get-tuple-element.177.refs_4_) | copy-start | bytes 2359300
  227.1 7.0 %copy-start.15 = (bf16[256,768]{1,0:T(8,128)(2,1)S(1)}, bf16[256,768]{1,0:T(8,128)(2,1)}, u32[]{:S(2)}) copy-start(bf16[256,768]{1,0:T(8,128)(2,1)} %get-tuple-element.178.refs_5_) | copy-start | bytes 1179652
  229.0 34.5 %collective-permute-start.14 = (bf16[4,240,768]{2,1,0:T(8,128)(2,1)S(1)}, bf16[4,240,768]{2,1,0:T(8,128)(2,1)}, u32[]{:S(2)}, u32[]{:S(2)}) collective-permute-start(bf16[4,240,768]{2,1,0:T(8,128)(2,1)S(1)} %add_convert_fusion.1), channel_id=1, source_target_pairs={{0,2},{1,3},{2,0},{3,1},{4,6},{5,7},{6,4},{7,5},{8,10},{9,11},{10,... | collective-permute-start | bytes 4423688 | tf_op jit(solution)/shard_map/ppermute | solution.py:958
  229.7 33.9 %collective-permute-start.18 = (bf16[4,240,768]{2,1,0:T(8,128)(2,1)S(1)}, bf16[4,240,768]{2,1,0:T(8,128)(2,1)}, u32[]{:S(2)}, u32[]{:S(2)}) collective-permute-start(bf16[4,240,768]{2,1,0:T(8,128)(2,1)S(1)} %copy-done.35), channel_id=1, source_target_pairs={{0,1},{1,0},{2,3},{3,2},{4,5},{5,4},{6,7},{7,6},{8,9},{9,8},{10,11... | collective-permute-start | bytes 4423688 | tf_op jit(solution)/shard_map/ppermute | solution.py:958
  229.7 29.0 %collective-permute-start.15 = (bf16[2,96,768]{2,1,0:T(8,128)(2,1)S(1)}, bf16[2,96,768]{2,1,0:T(8,128)(2,1)S(1)}, u32[]{:S(2)}, u32[]{:S(2)}) collective-permute-start(bf16[2,96,768]{2,1,0:T(8,128)(2,1)S(1)} %get-tuple-element.174), channel_id=1, source_target_pairs={{0,12},{1,13},{2,14},{3,15},{4,8},{5,9},{6,10},{7,11},{8,4},{9,5},... | collective-permute-start | bytes 884744 | tf_op jit(solution)/shard_map/ppermute | solution.py:958
  231.0 27.7 %collective-permute-start.16 = (bf16[2,96,768]{2,1,0:T(8,128)(2,1)S(1)}, bf16[2,96,768]{2,1,0:T(8,128)(2,1)S(1)}, u32[]{:S(2)}, u32[]{:S(2)}) collective-permute-start(bf16[2,96,768]{2,1,0:T(8,128)(2,1)S(1)} %get-tuple-element.175), channel_id=1, source_target_pairs={{0,8},{1,9},{2,10},{3,11},{4,12},{5,13},{6,14},{7,15},{8,0},{9,1},... | collective-permute-start | bytes 884744 | tf_op jit(solution)/shard_map/ppermute | solution.py:958
  231.2 27.5 %collective-permute-start.17 = (bf16[2,96,768]{2,1,0:T(8,128)(2,1)S(1)}, bf16[2,96,768]{2,1,0:T(8,128)(2,1)S(1)}, u32[]{:S(2)}, u32[]{:S(2)}) collective-permute-start(bf16[2,96,768]{2,1,0:T(8,128)(2,1)S(1)} %get-tuple-element.176), channel_id=1, source_target_pairs={{0,4},{1,5},{2,6},{3,7},{4,0},{5,1},{6,2},{7,3},{8,12},{9,13},{10,... | collective-permute-start | bytes 884744 | tf_op jit(solution)/shard_map/ppermute | solution.py:958
  234.1 5.0 %copy-start.1 = (bf16[16,576,768]{2,1,0:T(8,128)(2,1)S(1)}, bf16[16,576,768]{2,1,0:T(8,128)(2,1)}, u32[]{:S(2)}) copy-start(bf16[16,576,768]{2,1,0:T(8,128)(2,1)} %copy-done) | copy-start | bytes 42467332
  249.7 14.7 %copy-start.21 = (bf16[2,96,768]{2,1,0:T(8,128)(2,1)S(1)}, bf16[2,96,768]{2,1,0:T(8,128)(2,1)}, u32[]{:S(2)}) copy-start(bf16[2,96,768]{2,1,0:T(8,128)(2,1)} %get-tuple-element.197) | copy-start | bytes 884740
  258.7 8.6 %copy-start.22 = (f32[2,2,4608]{2,1,0:T(2,128)S(1)}, f32[2,2,4608]{2,1,0:T(2,128)}, u32[]{:S(2)}) copy-start(f32[2,2,4608]{2,1,0:T(2,128)} %get-tuple-element.206) | copy-start | bytes 221188
  258.7 4.9 %copy-start.29 = (bf16[2,96,768]{2,1,0:T(8,128)(2,1)}, bf16[2,96,768]{2,1,0:T(8,128)(2,1)S(1)}, u32[]{:S(2)}) copy-start(bf16[2,96,768]{2,1,0:T(8,128)(2,1)S(1)} %collective-permute-done.15) | copy-start | bytes 884740
  258.7 4.8 %copy-start.30 = (bf16[2,96,768]{2,1,0:T(8,128)(2,1)}, bf16[2,96,768]{2,1,0:T(8,128)(2,1)S(1)}, u32[]{:S(2)}) copy-start(bf16[2,96,768]{2,1,0:T(8,128)(2,1)S(1)} %collective-permute-done.16) | copy-start | bytes 884740
  258.7 4.8 %copy-start.31 = (bf16[2,96,768]{2,1,0:T(8,128)(2,1)}, bf16[2,96,768]{2,1,0:T(8,128)(2,1)S(1)}, u32[]{:S(2)}) copy-start(bf16[2,96,768]{2,1,0:T(8,128)(2,1)S(1)} %collective-permute-done.17) | copy-start | bytes 884740
  263.6 3.7 %collective-permute-start.19 = (bf16[4,240,768]{2,1,0:T(8,128)(2,1)}, bf16[4,240,768]{2,1,0:T(8,128)(2,1)}, u32[]{:S(2)}, u32[]{:S(2)}) collective-permute-start(bf16[4,240,768]{2,1,0:T(8,128)(2,1)} %get-tuple-element.196), channel_id=1, source_target_pairs={{0,1},{1,0},{2,3},{3,2},{4,5},{5,4},{6,7},{7,6},{8,9},{9,8},{10,11... | collective-permute-start | bytes 4423688 | tf_op jit(solution)/shard_map/ppermute | solution.py:958
  263.8 21.1 %collective-permute-start.24 = (bf16[4,240,768]{2,1,0:T(8,128)(2,1)}, bf16[4,240,768]{2,1,0:T(8,128)(2,1)}, u32[]{:S(2)}, u32[]{:S(2)}) collective-permute-start(bf16[4,240,768]{2,1,0:T(8,128)(2,1)} %copy-done.17), channel_id=1, source_target_pairs={{0,1},{1,0},{2,3},{3,2},{4,5},{5,4},{6,7},{7,6},{8,9},{9,8},{10,11... | collective-permute-start | bytes 4423688 | tf_op jit(solution)/shard_map/ppermute | solution.py:958
  267.4 14.5 %collective-permute-start.32 = (bf16[96,768]{1,0:T(8,128)(2,1)}, bf16[96,768]{1,0:T(8,128)(2,1)}, u32[]{:S(2)}, u32[]{:S(2)}) collective-permute-start(bf16[96,768]{1,0:T(8,128)(2,1)} %fusion.17), channel_id=1, source_target_pairs={{0,2},{1,3},{2,0},{3,1},{4,6},{5,7},{6,4},{7,5},{8,10},{9,11},{10,... | collective-permute-start | bytes 442376 | tf_op jit(solution)/shard_map/ppermute | solution.py:958
  268.1 6.5 %copy-start.20 = (bf16[4,240,768]{2,1,0:T(8,128)(2,1)S(1)}, bf16[4,240,768]{2,1,0:T(8,128)(2,1)}, u32[]{:S(2)}) copy-start(bf16[4,240,768]{2,1,0:T(8,128)(2,1)} %get-tuple-element.185) | copy-start | bytes 4423684
  268.1 5.9 %collective-permute-start.25 = (bf16[1,3,4608]{2,1,0:T(4,128)(2,1)S(1)}, bf16[1,3,4608]{2,1,0:T(4,128)(2,1)S(1)}, u32[]{:S(2)}, u32[]{:S(2)}) collective-permute-start(bf16[1,3,4608]{2,1,0:T(4,128)(2,1)S(1)} %pad_maximum_fusion.6), channel_id=1, source_target_pairs={{0,8},{1,9},{2,10},{3,11},{4,12},{5,13},{6,14},{7,15},{8,0},{9,1},... | collective-permute-start | bytes 82952 | tf_op jit(solution)/shard_map/ppermute | solution.py:958
  272.5 39.9 %collective-permute-start.23 = (bf16[4,240,768]{2,1,0:T(8,128)(2,1)}, bf16[4,240,768]{2,1,0:T(8,128)(2,1)S(1)}, u32[]{:S(2)}, u32[]{:S(2)}) collective-permute-start(bf16[4,240,768]{2,1,0:T(8,128)(2,1)} %add_convert_fusion), channel_id=1, source_target_pairs={{0,2},{1,3},{2,0},{3,1},{4,6},{5,7},{6,4},{7,5},{8,10},{9,11},{10,... | collective-permute-start | bytes 4423688 | tf_op jit(solution)/shard_map/ppermute | solution.py:958
  274.1 6.1 %collective-permute-start.26 = (bf16[2,3,4608]{2,1,0:T(4,128)(2,1)S(1)}, bf16[2,3,4608]{2,1,0:T(4,128)(2,1)S(1)}, u32[]{:S(2)}, u32[]{:S(2)}) collective-permute-start(bf16[2,3,4608]{2,1,0:T(4,128)(2,1)S(1)} %maximum_bitcast_fusion.2), channel_id=1, source_target_pairs={{0,4},{1,5},{2,6},{3,7},{4,0},{5,1},{6,2},{7,3},{8,12},{9,13},{10,... | collective-permute-start | bytes 165896 | tf_op jit(solution)/shard_map/ppermute | solution.py:958
  277.8 13.7 %collective-permute-start.20 = (bf16[240,768]{1,0:T(8,128)(2,1)}, bf16[240,768]{1,0:T(8,128)(2,1)}, u32[]{:S(2)}, u32[]{:S(2)}) collective-permute-start(bf16[240,768]{1,0:T(8,128)(2,1)} %get-tuple-element.243), channel_id=1, source_target_pairs={{0,12},{1,13},{2,14},{3,15},{4,8},{5,9},{6,10},{7,11},{8,4},{9,5},... | collective-permute-start | bytes 1105928 | tf_op jit(solution)/shard_map/ppermute | solution.py:958
  280.2 32.1 %collective-permute-start.21 = (bf16[240,768]{1,0:T(8,128)(2,1)}, bf16[240,768]{1,0:T(8,128)(2,1)}, u32[]{:S(2)}, u32[]{:S(2)}) collective-permute-start(bf16[240,768]{1,0:T(8,128)(2,1)} %get-tuple-element.242), channel_id=1, source_target_pairs={{0,8},{1,9},{2,10},{3,11},{4,12},{5,13},{6,14},{7,15},{8,0},{9,1},... | collective-permute-start | bytes 1105928 | tf_op jit(solution)/shard_map/ppermute | solution.py:958
  281.9 30.5 %collective-permute-start.22 = (bf16[240,768]{1,0:T(8,128)(2,1)}, bf16[240,768]{1,0:T(8,128)(2,1)S(1)}, u32[]{:S(2)}, u32[]{:S(2)}) collective-permute-start(bf16[240,768]{1,0:T(8,128)(2,1)} %get-tuple-element.241), channel_id=1, source_target_pairs={{0,4},{1,5},{2,6},{3,7},{4,0},{5,1},{6,2},{7,3},{8,12},{9,13},{10,... | collective-permute-start | bytes 1105928 | tf_op jit(solution)/shard_map/ppermute | solution.py:958
  312.4 7.5 %copy-start.19 = (bf16[4,240,768]{2,1,0:T(8,128)(2,1)}, bf16[4,240,768]{2,1,0:T(8,128)(2,1)S(1)}, u32[]{:S(2)}) copy-start(bf16[4,240,768]{2,1,0:T(8,128)(2,1)S(1)} %collective-permute-done.23) | copy-start | bytes 4423684
  312.4 7.5 %copy-start.28 = (bf16[4,3,4608]{2,0,1:T(4,128)(2,1)S(1)}, bf16[4,3,4608]{2,0,1:T(4,128)(2,1)}, u32[]{:S(2)}) copy-start(bf16[4,3,4608]{2,0,1:T(4,128)(2,1)} %reshape.214) | copy-start | bytes 331780
  315.5 13.7 %collective-permute-start.29 = (bf16[240,768]{1,0:T(8,128)(2,1)}, bf16[240,768]{1,0:T(8,128)(2,1)}, u32[]{:S(2)}, u32[]{:S(2)}) collective-permute-start(bf16[240,768]{1,0:T(8,128)(2,1)} %get-tuple-element.238), channel_id=1, source_target_pairs={{0,12},{1,13},{2,14},{3,15},{4,8},{5,9},{6,10},{7,11},{8,4},{9,5},... | collective-permute-start | bytes 1105928 | tf_op jit(solution)/shard_map/ppermute | solution.py:958
  316.6 30.3 %collective-permute-start.30 = (bf16[240,768]{1,0:T(8,128)(2,1)}, bf16[240,768]{1,0:T(8,128)(2,1)}, u32[]{:S(2)}, u32[]{:S(2)}) collective-permute-start(bf16[240,768]{1,0:T(8,128)(2,1)} %get-tuple-element.240), channel_id=1, source_target_pairs={{0,8},{1,9},{2,10},{3,11},{4,12},{5,13},{6,14},{7,15},{8,0},{9,1},... | collective-permute-start | bytes 1105928 | tf_op jit(solution)/shard_map/ppermute | solution.py:958
  316.6 30.3 %collective-permute-start.31 = (bf16[240,768]{1,0:T(8,128)(2,1)}, bf16[240,768]{1,0:T(8,128)(2,1)}, u32[]{:S(2)}, u32[]{:S(2)}) collective-permute-start(bf16[240,768]{1,0:T(8,128)(2,1)} %get-tuple-element.239), channel_id=1, source_target_pairs={{0,4},{1,5},{2,6},{3,7},{4,0},{5,1},{6,2},{7,3},{8,12},{9,13},{10,... | collective-permute-start | bytes 1105928 | tf_op jit(solution)/shard_map/ppermute | solution.py:958
  319.9 4.7 %collective-permute-start.27 = (bf16[4,3,4608]{2,0,1:T(4,128)(2,1)S(1)}, bf16[4,3,4608]{2,0,1:T(4,128)(2,1)S(1)}, u32[]{:S(2)}, u32[]{:S(2)}) collective-permute-start(bf16[4,3,4608]{2,0,1:T(4,128)(2,1)S(1)} %copy-done.28), channel_id=1, source_target_pairs={{0,2},{1,3},{2,0},{3,1},{4,6},{5,7},{6,4},{7,5},{8,10},{9,11},{10,... | collective-permute-start | bytes 331784 | tf_op jit(solution)/shard_map/ppermute | solution.py:958
  325.1 1.5 collective-permute-start.28
  (6 other events, 6.6 us)
Sparse Core Ops, SparseCore 0:
  10.9 116.6 all-gather.2

commit v2 on v1

--- a/solution.py
+++ b/solution.py
@@ -931,8 +931,8 @@
     far0 = add(far0, swap(core0[1], 1)).astype(bf16)
     terms2 = line_terms(z, both2, swap(core2, 1))
 
-    far0, terms2, near_core0 = meet((far0, terms2, core0[0]))
-    group1, small = second((far0, terms2))
+    *ready, near_core0 = meet((far0, terms2, core0[0]))
+    group1, small = second(ready)
     far0, terms2 = swap(far0, 2), line_swap(terms2)
     core0 = swap(near_core0, 1)
 

time: 364 us -> 365 us (level)
  no operation moved by 1% of the time
where the time goes in v2:
time: 365 us; the launch traced here: 358 us
  waiting for transfers between devices  182 us (50%)
  Pallas kernels  82.5 us (23%)
  starting transfers between devices  37.6 us (10%)
  other arithmetic  23.2 us (6%)
  local copies, waits for them, and re-layouts  15.9 us (4%)
  between operations  15 us (4%)
    ppermute x29, waiting for transfers between devices, swap(): return lax.ppermute(block, DP, [(i, i ^ distance) for i in range(count)])  92 us
    all_gather x1, waiting for transfers between devices, local(): weights = lax.all_gather(shard, DP, axis=0, tiled=False)  67.7 us
    pallas_call x7, Pallas kernels, call(): pl.pallas_call(lambda *refs: kernel(c, micro, names, refs), out_shape=sha...  65 us
    ppermute x29, starting transfers between devices, swap(): return lax.ppermute(block, DP, [(i, i ^ distance) for i in range(count)])  32.1 us
    pallas_call x2, Pallas kernels, weight_gradients(): pl.pallas_call(partial(gradients_kernel, c, ring, order), out_shape=out,...  17.5 us
    ppermute x2, waiting for transfers between devices, local(): grads.append(in_vmem(lax.ppermute(got[N.send], SECTION, [(1, 0)])))  15.2 us
    convert_element_type x3, other arithmetic, line_terms(): add(*[at(part, k) for part in parts]).astype(bf16)  8.55 us
    unnamed x80, local copies, waits for them, and re-layouts  7.34 us
  transfers between devices with their start and end apart: 34, of which 21 were waited for; matrix products, arithmetic and copies ran while one was open for 7% of the time, Pallas kernels for 14%

profile of v2, /device:TPU:0, one launch (start us, length us, event | category | flops | bytes accessed | tf_op | source)
XLA Modules:
  0.0 357.8 jit_solution(3734276404363082647)
XLA Ops:
  7.2 1.1 convert_bitcast_fusion.1
  8.7 0.9 copy-done.23
  9.6 4.1 %collective-permute-start = (s32[1,2]{1,0:T(1,128)S(1)}, s32[1,2]{1,0:T(1,128)S(1)}, u32[]{:S(2)}, u32[]{:S(2)}) collective-permute-start(s32[1,2]{1,0:T(1,128)S(1)} %bitcast.147), channel_id=1, source_target_pairs={{0,8},{1,9},{2,10},{3,11},{4,12},{5,13},{6,14},{7,15},{8,0},{9,1},... | collective-permute-start | bytes 32 | tf_op jit(solution)/shard_map/ppermute | solution.py:958
  13.7 1.5 collective-permute-done
  15.2 2.0 collective-permute-start.1
  17.2 1.7 collective-permute-done.1
  19.1 1.8 collective-permute-start.2
  20.9 1.7 collective-permute-done.2
  22.8 1.1 collective-permute-done.3
  25.7 1.6 collective-permute-done.4
  28.1 1.9 collective-permute-start.5
  30.2 8.6 %collective-permute-done.5 = f32[4,3,4608]{2,0,1:T(4,128)S(1)} collective-permute-done((f32[4,3,4608]{2,0,1:T(4,128)S(1)}, f32[4,3,4608]{2,0,1:T(4,128)S(1)}, u32[]{:S(2)}, u32[]{:S(2)}) %collective-permute-start.5) | collective-permute-done | bytes 221216 | tf_op jit(solution)/shard_map/ppermute | solution.py:958
  39.9 1.6 collective-permute-start.6
  41.5 12.0 %collective-permute-done.6 = f32[2,3,4608]{2,0,1:T(2,128)S(1)} collective-permute-done((f32[2,3,4608]{2,0,1:T(2,128)S(1)}, f32[2,3,4608]{2,0,1:T(2,128)S(1)}, u32[]{:S(2)}, u32[]{:S(2)}) %collective-permute-start.6) | collective-permute-done | bytes 110624 | tf_op jit(solution)/shard_map/ppermute | solution.py:958
  54.4 5.3 %collective-permute-done.7 = f32[1,3,4608]{2,0,1:T(1,128)S(1)} collective-permute-done((f32[1,3,4608]{2,0,1:T(1,128)S(1)}, f32[1,3,4608]{2,0,1:T(1,128)S(1)}, u32[]{:S(2)}, u32[]{:S(2)}) %collective-permute-start.7) | collective-permute-done | bytes 55328 | tf_op jit(solution)/shard_map/ppermute | solution.py:958
  59.9 67.7 %all-gather.3.cloned.1.call-done = bf16[9216,768]{1,0:T(8,128)(2,1)} async-done(((bf16[576,768]{1,0:T(8,128)(2,1)}), bf16[9216,768]{1,0:T(8,128)(2,1)}) %all-gather.3.cloned.1.call-update) | async-done | bytes 14155792 | tf_op jit(solution)/shard_map/all_gather | solution.py:1037
  127.6 13.7 %shard_map.144 = (bf16[256,768]{1,0:T(8,128)(2,1)S(1)}, bf16[256,2304]{1,0:T(8,128)(2,1)}, bf16[256,768]{1,0:T(8,128)(2,1)}, f32[256,768]{1,0:T(8,128)}, f32[256...) custom-call(s32[9]{0:T(128)S(1)} %pad_add_fusion.4.refs_0_, ...), custom_call_target="tpu_custom_call" | custom-call | flops 3623878656 | bytes 20000000 | tf_op jit(solution)/shard_map/pallas_call | solution.py:742
  141.3 1.3 collective-permute-start.9
  142.7 12.7 %shard_map.145 = (f32[2,256,768]{2,1,0:T(8,128)}, bf16[256,768]{1,0:T(8,128)(2,1)S(1)}, bf16[256,2304]{1,0:T(8,128)(2,1)}, bf16[256,768]{1,0:T(8,128)(2,1)}, f32...) custom-call(s32[9]{0:T(128)S(1)} %pad_add_fusion.3.refs_0_, ...), custom_call_target="tpu_custom_call", output_to_operand_aliasing={{0}: (4, {})} | custom-call | flops 3623878656 | bytes 20000000 | tf_op jit(solution)/shard_map/pallas_call | solution.py:742
  155.5 1.3 collective-permute-start.8
  156.8 1.0 shard_map.146
  157.8 1.3 collective-permute-start.11
  159.1 6.7 %collective-permute-done.8.refs_1_ = bf16[256,768]{1,0:T(8,128)(2,1)S(1)} collective-permute-done((bf16[256,768]{1,0:T(8,128)(2,1)S(1)}, bf16[256,768]{1,0:T(8,128)(2,1)S(1)}, u32[]{:S(2)}, u32[]{:S(2)}) %collective-permute-start.8) | collective-permute-done | bytes 393248 | tf_op jit(solution)/shard_map/ppermute | solution.py:1096
  165.9 1.1 shard_map.147
  166.9 1.6 collective-permute-start.10
  168.5 13.7 %collective-permute-done.11.refs_3_ = bf16[256,768]{1,0:T(8,128)(2,1)S(1)} collective-permute-done((bf16[256,768]{1,0:T(8,128)(2,1)S(1)}, bf16[256,768]{1,0:T(8,128)(2,1)S(1)}, u32[]{:S(2)}, u32[]{:S(2)}) %collective-permute-start.11) | collective-permute-done | bytes 393248 | tf_op jit(solution)/shard_map/ppermute | solution.py:1118
  182.3 17.1 %shard_map.148 = (f32[2,256,768]{2,1,0:T(8,128)}, f32[2,2,4608]{2,1,0:T(2,128)}, bf16[512,768]{1,0:T(8,128)(2,1)}, bf16[512,2304]{1,0:T(8,128)(2,1)}, bf16[512,7...) custom-call(s32[9]{0:T(128)S(1)} %pad_add_fusion.4.refs_0_, ...), custom_call_target="tpu_custom_call", output_to_operand_aliasing={{0}: (11, {}), {1}: (12, {}), {2}: (13, {}), {3}: (14, {}),... | custom-call | flops 7247757312 | bytes 20000000 | tf_op jit(solution)/shard_map/pallas_call | solution.py:742
  199.4 1.5 collective-permute-done.10.refs_3_
  200.9 8.9 %shard_map.149 = (f32[2,2,4608]{2,1,0:T(2,128)}, bf16[512,768]{1,0:T(8,128)(2,1)}, bf16[512,3072]{1,0:T(8,128)(2,1)}, bf16[512,3072]{1,0:T(8,128)(2,1)}, bf16[51...) custom-call(s32[9]{0:T(128)S(1)} %pad_add_fusion.3.refs_0_, ...), custom_call_target="tpu_custom_call", output_to_operand_aliasing={{0}: (9, {}), {1}: (10, {}), {2}: (11, {}), {3}: (12, {}), ... | custom-call | flops 4831838208 | bytes 20000000 | tf_op jit(solution)/shard_map/pallas_call | solution.py:742
  209.8 9.6 %shard_map.151 = (bf16[4,240,768]{2,1,0:T(8,128)(2,1)}, bf16[4,240,768]{2,1,0:T(8,128)(2,1)S(1)}, bf16[4,240,768]{2,1,0:T(8,128)(2,1)}, bf16[4,240,768]{2,1,0:T(...) custom-call(s32[2]{0:T(128)S(1)} %pad_add_fusion.5.place, ...), custom_call_target="tpu_custom_call" | custom-call | flops 4227858432 | bytes 12000000 | tf_op jit(solution)/shard_map/pallas_call | solution.py:890
  220.0 4.8 %collective-permute-done.14 = bf16[4,2,96,768]{3,2,1,0:T(8,128)(2,1)} collective-permute-done((bf16[4,2,96,768]{3,2,1,0:T(8,128)(2,1)}, bf16[4,2,96,768]{3,2,1,0:T(8,128)(2,1)}, u32[]{:S(2)}, u32[]{:S(2)}) %collective-permute-start.14) | collective-permute-done | bytes 1179680 | tf_op jit(solution)/shard_map/ppermute | solution.py:958
  224.8 2.3 fusion.16
  227.1 2.0 add_convert_fusion.1
  229.8 1.3 collective-permute-start.15
  231.3 2.9 collective-permute-start.17
  234.2 5.0 %copy-done.1 = bf16[16,576,768]{2,1,0:T(8,128)(2,1)S(1)} copy-done((bf16[16,576,768]{2,1,0:T(8,128)(2,1)S(1)}, bf16[16,576,768]{2,1,0:T(8,128)(2,1)}, u32[]{:S(2)}) %copy-start.1) | copy-done | bytes 14155800
  239.3 10.5 %shard_map.150 = (f32[2,256,768]{2,1,0:T(8,128)}, f32[2,2,4608]{2,1,0:T(2,128)}, bf16[512,2304]{1,0:T(8,128)(2,1)}, bf16[512,768]{1,0:T(8,128)(2,1)}) custom-call(s32[9]{0:T(128)S(1)} %pad_add_fusion.3.refs_0_, f32[2,2,4608]{2,1,0:T(2,128)S(1)} %pad_maximum_fusion.3.refs_2_.refs_1_, ...), custom_call_target="tpu_custom_call", output_to_operand_aliasing={{0}: (7, {}), {1}: (8, {}), {2}: (9, {}), {3}: (10, {})} | custom-call | flops 2415919104 | bytes 20000000 | tf_op jit(solution)/shard_map/pallas_call | solution.py:742
  249.8 7.9 %shard_map.152 = (bf16[4,240,768]{2,1,0:T(8,128)(2,1)S(1)}, bf16[4,240,768]{2,1,0:T(8,128)(2,1)S(1)}, bf16[4,240,768]{2,1,0:T(8,128)(2,1)S(1)}, bf16[4,240,768]{2,1,0:T(8,128)(2,1)}) custom-call(s32[2]{0:T(128)S(1)} %pad_add_fusion.5.place, bf16[512,768]{1,0:T(8,128)(2,1)} %get-tuple-element.166.refs_2_.refs_0_, ...), custom_call_target="tpu_custom_call" | custom-call | flops 3019898880 | bytes 12000000 | tf_op jit(solution)/shard_map/pallas_call | solution.py:890
  257.7 1.1 copy-done.17
  258.9 5.0 %collective-permute-done.13 = bf16[4,240,768]{2,1,0:T(8,128)(2,1)} collective-permute-done((bf16[4,240,768]{2,1,0:T(8,128)(2,1)S(1)}, bf16[4,240,768]{2,1,0:T(8,128)(2,1)}, u32[]{:S(2)}, u32[]{:S(2)}) %collective-permute-start.13) | collective-permute-done | bytes 1474592 | tf_op jit(solution)/shard_map/ppermute | solution.py:958
  264.8 1.3 convert_add_fusion.2
  266.7 0.7 slice_bitcast_fusion.1
  268.5 1.6 collective-permute-start.25
  270.0 2.9 add_convert_fusion
  272.9 1.5 collective-permute-start.23
  275.0 3.2 fusion.8
  278.2 2.4 collective-permute-start.20
  281.5 0.7 reshape.214
  282.2 1.3 collective-permute-start.22
  283.6 1.0 convert_add_fusion.3
  285.3 6.6 %collective-permute-done.20 = bf16[240,768]{1,0:T(8,128)(2,1)} collective-permute-done((bf16[240,768]{1,0:T(8,128)(2,1)}, bf16[240,768]{1,0:T(8,128)(2,1)}, u32[]{:S(2)}, u32[]{:S(2)}) %collective-permute-start.20) | collective-permute-done | bytes 368672 | tf_op jit(solution)/shard_map/ppermute | solution.py:958
  291.9 20.8 %collective-permute-done.21 = bf16[240,768]{1,0:T(8,128)(2,1)} collective-permute-done((bf16[240,768]{1,0:T(8,128)(2,1)}, bf16[240,768]{1,0:T(8,128)(2,1)}, u32[]{:S(2)}, u32[]{:S(2)}) %collective-permute-start.21) | collective-permute-done | bytes 368672 | tf_op jit(solution)/shard_map/ppermute | solution.py:958
  312.7 3.1 fusion.10
  315.8 1.2 collective-permute-start.29
  317.0 3.2 collective-permute-start.31
  320.8 1.3 convert_add_fusion.1
  322.1 0.9 slice_bitcast_fusion
  322.9 2.1 collective-permute-done.27
  326.3 0.8 collective-permute-done.28
  327.8 1.4 convolution_bitcast_fusion
  329.6 17.7 %collective-permute-done.30 = bf16[240,768]{1,0:T(8,128)(2,1)} collective-permute-done((bf16[240,768]{1,0:T(8,128)(2,1)}, bf16[240,768]{1,0:T(8,128)(2,1)}, u32[]{:S(2)}, u32[]{:S(2)}) %collective-permute-start.30) | collective-permute-done | bytes 368672 | tf_op jit(solution)/shard_map/ppermute | solution.py:958
  347.3 1.7 fusion.1
  349.1 0.8 maximum_bitcast_fusion.1
  349.9 0.9 maximum_bitcast_fusion
  (177 shorter events, 14.9 us)
Async XLA Ops:
  7.2 1.4 copy-start.27
  7.2 120.4 %all-gather.3.cloned.1.call-start = ((), (), s32[]{:S(2)}) async-start(), calls=%async_computation | async-start | bytes 15040512 | tf_op jit(solution)/shard_map/all_gather | solution.py:1037
  8.5 15.7 %copy-start.24 = (f32[1,48,4608]{2,1,0:T(8,128)S(1)}, f32[1,48,4608]{2,1,0:T(8,128)}, u32[]{:S(2)}) copy-start(f32[1,48,4608]{2,1,0:T(8,128)} %param.13) | copy-start | bytes 2654212
  9.6 5.6 %collective-permute-start = (s32[1,2]{1,0:T(1,128)S(1)}, s32[1,2]{1,0:T(1,128)S(1)}, u32[]{:S(2)}, u32[]{:S(2)}) collective-permute-start(s32[1,2]{1,0:T(1,128)S(1)} %bitcast.147), channel_id=1, source_target_pairs={{0,8},{1,9},{2,10},{3,11},{4,12},{5,13},{6,14},{7,15},{8,0},{9,1},... | collective-permute-start | bytes 32 | tf_op jit(solution)/shard_map/ppermute | solution.py:958
  15.2 3.6 %collective-permute-start.1 = (s32[2,2]{1,0:T(2,128)S(1)}, s32[2,2]{1,0:T(2,128)S(1)}, u32[]{:S(2)}, u32[]{:S(2)}) collective-permute-start(s32[2,2]{1,0:T(2,128)S(1)} %add_bitcast_fusion), channel_id=1, source_target_pairs={{0,4},{1,5},{2,6},{3,7},{4,0},{5,1},{6,2},{7,3},{8,12},{9,13},{10,... | collective-permute-start | bytes 56 | tf_op jit(solution)/shard_map/ppermute | solution.py:958
  19.1 3.6 collective-permute-start.2
  22.8 1.1 collective-permute-start.3
  25.4 1.9 collective-permute-start.4
  25.7 4.3 %copy-start.33 = (s32[2,1,2,4]{3,2,1,0:T(2,128)S(1)}, s32[2,1,2,4]{3,2,1,0:T(2,128)}, u32[]{:S(2)}) copy-start(s32[2,1,2,4]{3,2,1,0:T(2,128)} %param.11) | copy-start | bytes 196
  28.1 10.7 %collective-permute-start.5 = (f32[4,3,4608]{2,0,1:T(4,128)S(1)}, f32[4,3,4608]{2,0,1:T(4,128)S(1)}, u32[]{:S(2)}, u32[]{:S(2)}) collective-permute-start(f32[4,3,4608]{2,0,1:T(4,128)S(1)} %broadcast_select_fusion.1), channel_id=1, source_target_pairs={{0,2},{1,3},{2,0},{3,1},{4,6},{5,7},{6,4},{7,5},{8,10},{9,11},{10,... | collective-permute-start | bytes 663560 | tf_op jit(solution)/shard_map/ppermute | solution.py:958
  30.1 97.5 %copy-start.2 = (bf16[2,1,2,128,768]{4,3,2,1,0:T(8,128)(2,1)S(1)}, bf16[2,1,2,128,768]{4,3,2,1,0:T(8,128)(2,1)}, u32[]{:S(2)}) copy-start(bf16[2,1,2,128,768]{4,3,2,1,0:T(8,128)(2,1)} %param.9) | copy-start | bytes 2359300
  39.9 13.6 %collective-permute-start.6 = (f32[2,3,4608]{2,0,1:T(2,128)S(1)}, f32[2,3,4608]{2,0,1:T(2,128)S(1)}, u32[]{:S(2)}, u32[]{:S(2)}) collective-permute-start(f32[2,3,4608]{2,0,1:T(2,128)S(1)} %broadcast_select_fusion.2), channel_id=1, source_target_pairs={{0,4},{1,5},{2,6},{3,7},{4,0},{5,1},{6,2},{7,3},{8,12},{9,13},{10,... | collective-permute-start | bytes 331784 | tf_op jit(solution)/shard_map/ppermute | solution.py:958
  53.7 6.0 %collective-permute-start.7 = (f32[1,3,4608]{2,0,1:T(1,128)S(1)}, f32[1,3,4608]{2,0,1:T(1,128)S(1)}, u32[]{:S(2)}, u32[]{:S(2)}) collective-permute-start(f32[1,3,4608]{2,0,1:T(1,128)S(1)} %broadcast_select_fusion.3), channel_id=1, source_target_pairs={{0,8},{1,9},{2,10},{3,11},{4,12},{5,13},{6,14},{7,15},{8,0},{9,1},... | collective-permute-start | bytes 165896 | tf_op jit(solution)/shard_map/ppermute | solution.py:958
  141.3 59.6 %copy-start = (bf16[16,576,768]{2,1,0:T(8,128)(2,1)}, bf16[16,576,768]{2,1,0:T(8,128)(2,1)S(1)}, u32[]{:S(2)}) copy-start(bf16[16,576,768]{2,1,0:T(8,128)(2,1)S(1)} %get-tuple-element.107.refs_3_.refs_2_) | copy-start | bytes 42467332
  141.3 15.5 %collective-permute-start.9 = (bf16[256,768]{1,0:T(8,128)(2,1)S(1)}, bf16[256,768]{1,0:T(8,128)(2,1)S(1)}, u32[]{:S(2)}, u32[]{:S(2)}) collective-permute-start(bf16[256,768]{1,0:T(8,128)(2,1)S(1)} %get-tuple-element.110), channel_id=1, source_target_pairs={{0,16},{1,17},{2,18},{3,19},{4,20},{5,21},{6,22},{7,23},{8,24},{9,... | collective-permute-start | bytes 1179656 | tf_op jit(solution)/shard_map/ppermute | solution.py:1096
  142.7 14.1 %copy-start.18 = (bf16[2,1,2,128,768]{4,3,2,1,0:T(8,128)(2,1)S(1)}, bf16[2,1,2,128,768]{4,3,2,1,0:T(8,128)(2,1)}, u32[]{:S(2)}) copy-start(bf16[2,1,2,128,768]{4,3,2,1,0:T(8,128)(2,1)} %param.10) | copy-start | bytes 2359300
  155.5 10.4 %collective-permute-start.8 = (bf16[256,768]{1,0:T(8,128)(2,1)S(1)}, bf16[256,768]{1,0:T(8,128)(2,1)S(1)}, u32[]{:S(2)}, u32[]{:S(2)}) collective-permute-start(bf16[256,768]{1,0:T(8,128)(2,1)S(1)} %get-tuple-element.109), channel_id=1, source_target_pairs={{0,16},{1,17},{2,18},{3,19},{4,20},{5,21},{6,22},{7,23},{8,24},{9,... | collective-permute-start | bytes 1179656 | tf_op jit(solution)/shard_map/ppermute | solution.py:1096
  157.8 24.4 %collective-permute-start.11 = (bf16[256,768]{1,0:T(8,128)(2,1)S(1)}, bf16[256,768]{1,0:T(8,128)(2,1)S(1)}, u32[]{:S(2)}, u32[]{:S(2)}) collective-permute-start(bf16[256,768]{1,0:T(8,128)(2,1)S(1)} %get-tuple-element.130), channel_id=1, source_target_pairs={{16,0},{17,1},{18,2},{19,3},{20,4},{21,5},{22,6},{23,7},{24,8},{25... | collective-permute-start | bytes 1179656 | tf_op jit(solution)/shard_map/ppermute | solution.py:1118
  165.8 16.4 %copy-start.3 = (f32[256,3072]{1,0:T(8,128)S(1)}, f32[256,3072]{1,0:T(8,128)}, u32[]{:S(2)}) copy-start(f32[256,3072]{1,0:T(8,128)} %get-tuple-element.135.refs_9_) | copy-start | bytes 9437188
  165.8 16.4 %copy-start.6 = (bf16[256,2304]{1,0:T(8,128)(2,1)S(1)}, bf16[256,2304]{1,0:T(8,128)(2,1)}, u32[]{:S(2)}) copy-start(bf16[256,2304]{1,0:T(8,128)(2,1)} %get-tuple-element.131.refs_5_) | copy-start | bytes 3538948
  165.8 16.4 %copy-start.8 = (f32[256,768]{1,0:T(8,128)S(1)}, f32[256,768]{1,0:T(8,128)}, u32[]{:S(2)}) copy-start(f32[256,768]{1,0:T(8,128)} %get-tuple-element.133.refs_7_) | copy-start | bytes 2359300
  165.8 16.4 %copy-start.9 = (f32[256,768]{1,0:T(8,128)S(1)}, f32[256,768]{1,0:T(8,128)}, u32[]{:S(2)}) copy-start(f32[256,768]{1,0:T(8,128)} %get-tuple-element.134.refs_8_) | copy-start | bytes 2359300
  165.8 16.4 %copy-start.10 = (f32[256,768]{1,0:T(8,128)S(1)}, f32[256,768]{1,0:T(8,128)}, u32[]{:S(2)}) copy-start(f32[256,768]{1,0:T(8,128)} %get-tuple-element.136.refs_10_) | copy-start | bytes 2359300
  165.8 16.4 %copy-start.14 = (bf16[256,768]{1,0:T(8,128)(2,1)S(1)}, bf16[256,768]{1,0:T(8,128)(2,1)}, u32[]{:S(2)}) copy-start(bf16[256,768]{1,0:T(8,128)(2,1)} %get-tuple-element.132.refs_6_) | copy-start | bytes 1179652
  166.9 34.0 %collective-permute-start.10 = (bf16[256,768]{1,0:T(8,128)(2,1)S(1)}, bf16[256,768]{1,0:T(8,128)(2,1)S(1)}, u32[]{:S(2)}, u32[]{:S(2)}) collective-permute-start(bf16[256,768]{1,0:T(8,128)(2,1)S(1)} %get-tuple-element.124), channel_id=1, source_target_pairs={{16,0},{17,1},{18,2},{19,3},{20,4},{21,5},{22,6},{23,7},{24,8},{25... | collective-permute-start | bytes 1179656 | tf_op jit(solution)/shard_map/ppermute | solution.py:1118
  182.2 18.7 %copy-start.4 = (f32[256,3072]{1,0:T(8,128)S(1)}, f32[256,3072]{1,0:T(8,128)}, u32[]{:S(2)}) copy-start(f32[256,3072]{1,0:T(8,128)} %get-tuple-element.126.refs_5_) | copy-start | bytes 9437188
  182.3 18.6 %copy-start.11 = (f32[256,768]{1,0:T(8,128)S(1)}, f32[256,768]{1,0:T(8,128)}, u32[]{:S(2)}) copy-start(f32[256,768]{1,0:T(8,128)} %get-tuple-element.128.refs_7_) | copy-start | bytes 2359300
  182.3 18.6 %copy-start.12 = (f32[256,768]{1,0:T(8,128)S(1)}, f32[256,768]{1,0:T(8,128)}, u32[]{:S(2)}) copy-start(f32[256,768]{1,0:T(8,128)} %get-tuple-element.127.refs_6_) | copy-start | bytes 2359300
  182.3 18.6 %copy-start.13 = (f32[256,768]{1,0:T(8,128)S(1)}, f32[256,768]{1,0:T(8,128)}, u32[]{:S(2)}) copy-start(f32[256,768]{1,0:T(8,128)} %get-tuple-element.125.refs_4_) | copy-start | bytes 2359300
  182.3 18.6 %copy-start.16 = (bf16[256,768]{1,0:T(8,128)(2,1)S(1)}, bf16[256,768]{1,0:T(8,128)(2,1)}, u32[]{:S(2)}) copy-start(bf16[256,768]{1,0:T(8,128)(2,1)} %get-tuple-element.129.refs_8_) | copy-start | bytes 1179652
  219.4 7.6 %collective-permute-start.12 = (bf16[4,240,768]{2,1,0:T(8,128)(2,1)}, bf16[4,240,768]{2,1,0:T(8,128)(2,1)}, u32[]{:S(2)}, u32[]{:S(2)}) collective-permute-start(bf16[4,240,768]{2,1,0:T(8,128)(2,1)} %get-tuple-element.172), channel_id=1, source_target_pairs={{0,1},{1,0},{2,3},{3,2},{4,5},{5,4},{6,7},{7,6},{8,9},{9,8},{10,11... | collective-permute-start | bytes 4423688 | tf_op jit(solution)/shard_map/ppermute | solution.py:958
  219.5 5.3 %collective-permute-start.14 = (bf16[4,2,96,768]{3,2,1,0:T(8,128)(2,1)}, bf16[4,2,96,768]{3,2,1,0:T(8,128)(2,1)}, u32[]{:S(2)}, u32[]{:S(2)}) collective-permute-start(bf16[4,2,96,768]{3,2,1,0:T(8,128)(2,1)} %get-tuple-element.174), channel_id=1, source_target_pairs={{0,1},{1,0},{2,3},{3,2},{4,5},{5,4},{6,7},{7,6},{8,9},{9,8},{10,11... | collective-permute-start | bytes 3538952 | tf_op jit(solution)/shard_map/ppermute | solution.py:958
  227.1 2.0 copy-start.35
  227.1 7.2 %copy-start.5 = (bf16[256,2304]{1,0:T(8,128)(2,1)S(1)}, bf16[256,2304]{1,0:T(8,128)(2,1)}, u32[]{:S(2)}) copy-start(bf16[256,2304]{1,0:T(8,128)(2,1)} %get-tuple-element.158.refs_6_) | copy-start | bytes 3538948
  227.1 7.2 %copy-start.7 = (f32[256,768]{1,0:T(8,128)S(1)}, f32[256,768]{1,0:T(8,128)}, u32[]{:S(2)}) copy-start(f32[256,768]{1,0:T(8,128)} %get-tuple-element.156.refs_4_) | copy-start | bytes 2359300
  227.1 7.2 %copy-start.15 = (bf16[256,768]{1,0:T(8,128)(2,1)S(1)}, bf16[256,768]{1,0:T(8,128)(2,1)}, u32[]{:S(2)}) copy-start(bf16[256,768]{1,0:T(8,128)(2,1)} %get-tuple-element.157.refs_5_) | copy-start | bytes 1179652
  229.1 29.8 %collective-permute-start.18 = (bf16[4,240,768]{2,1,0:T(8,128)(2,1)S(1)}, bf16[4,240,768]{2,1,0:T(8,128)(2,1)}, u32[]{:S(2)}, u32[]{:S(2)}) collective-permute-start(bf16[4,240,768]{2,1,0:T(8,128)(2,1)S(1)} %copy-done.35), channel_id=1, source_target_pairs={{0,1},{1,0},{2,3},{3,2},{4,5},{5,4},{6,7},{7,6},{8,9},{9,8},{10,11... | collective-permute-start | bytes 4423688 | tf_op jit(solution)/shard_map/ppermute | solution.py:958
  229.3 34.7 %collective-permute-start.13 = (bf16[4,240,768]{2,1,0:T(8,128)(2,1)S(1)}, bf16[4,240,768]{2,1,0:T(8,128)(2,1)}, u32[]{:S(2)}, u32[]{:S(2)}) collective-permute-start(bf16[4,240,768]{2,1,0:T(8,128)(2,1)S(1)} %add_convert_fusion.1), channel_id=1, source_target_pairs={{0,2},{1,3},{2,0},{3,1},{4,6},{5,7},{6,4},{7,5},{8,10},{9,11},{10,... | collective-permute-start | bytes 4423688 | tf_op jit(solution)/shard_map/ppermute | solution.py:958
  229.8 29.0 %collective-permute-start.15 = (bf16[2,96,768]{2,1,0:T(8,128)(2,1)S(1)}, bf16[2,96,768]{2,1,0:T(8,128)(2,1)S(1)}, u32[]{:S(2)}, u32[]{:S(2)}) collective-permute-start(bf16[2,96,768]{2,1,0:T(8,128)(2,1)S(1)} %get-tuple-element.237), channel_id=1, source_target_pairs={{0,12},{1,13},{2,14},{3,15},{4,8},{5,9},{6,10},{7,11},{8,4},{9,5},... | collective-permute-start | bytes 884744 | tf_op jit(solution)/shard_map/ppermute | solution.py:958
  231.1 27.7 %collective-permute-start.16 = (bf16[2,96,768]{2,1,0:T(8,128)(2,1)S(1)}, bf16[2,96,768]{2,1,0:T(8,128)(2,1)S(1)}, u32[]{:S(2)}, u32[]{:S(2)}) collective-permute-start(bf16[2,96,768]{2,1,0:T(8,128)(2,1)S(1)} %get-tuple-element.236), channel_id=1, source_target_pairs={{0,8},{1,9},{2,10},{3,11},{4,12},{5,13},{6,14},{7,15},{8,0},{9,1},... | collective-permute-start | bytes 884744 | tf_op jit(solution)/shard_map/ppermute | solution.py:958
  231.3 27.5 %collective-permute-start.17 = (bf16[2,96,768]{2,1,0:T(8,128)(2,1)S(1)}, bf16[2,96,768]{2,1,0:T(8,128)(2,1)S(1)}, u32[]{:S(2)}, u32[]{:S(2)}) collective-permute-start(bf16[2,96,768]{2,1,0:T(8,128)(2,1)S(1)} %get-tuple-element.235), channel_id=1, source_target_pairs={{0,4},{1,5},{2,6},{3,7},{4,0},{5,1},{6,2},{7,3},{8,12},{9,13},{10,... | collective-permute-start | bytes 884744 | tf_op jit(solution)/shard_map/ppermute | solution.py:958
  234.2 5.0 %copy-start.1 = (bf16[16,576,768]{2,1,0:T(8,128)(2,1)S(1)}, bf16[16,576,768]{2,1,0:T(8,128)(2,1)}, u32[]{:S(2)}) copy-start(bf16[16,576,768]{2,1,0:T(8,128)(2,1)} %copy-done) | copy-start | bytes 42467332
  249.8 15.0 %copy-start.21 = (bf16[2,96,768]{2,1,0:T(8,128)(2,1)S(1)}, bf16[2,96,768]{2,1,0:T(8,128)(2,1)}, u32[]{:S(2)}) copy-start(bf16[2,96,768]{2,1,0:T(8,128)(2,1)} %get-tuple-element.187) | copy-start | bytes 884740
  258.8 8.8 %copy-start.22 = (f32[2,2,4608]{2,1,0:T(2,128)S(1)}, f32[2,2,4608]{2,1,0:T(2,128)}, u32[]{:S(2)}) copy-start(f32[2,2,4608]{2,1,0:T(2,128)} %get-tuple-element.196) | copy-start | bytes 221188
  258.8 5.1 %copy-start.29 = (bf16[2,96,768]{2,1,0:T(8,128)(2,1)}, bf16[2,96,768]{2,1,0:T(8,128)(2,1)S(1)}, u32[]{:S(2)}) copy-start(bf16[2,96,768]{2,1,0:T(8,128)(2,1)S(1)} %collective-permute-done.15) | copy-start | bytes 884740
  258.9 5.1 %copy-start.30 = (bf16[2,96,768]{2,1,0:T(8,128)(2,1)}, bf16[2,96,768]{2,1,0:T(8,128)(2,1)S(1)}, u32[]{:S(2)}) copy-start(bf16[2,96,768]{2,1,0:T(8,128)(2,1)S(1)} %collective-permute-done.16) | copy-start | bytes 884740
  258.9 5.1 %copy-start.31 = (bf16[2,96,768]{2,1,0:T(8,128)(2,1)}, bf16[2,96,768]{2,1,0:T(8,128)(2,1)S(1)}, u32[]{:S(2)}) copy-start(bf16[2,96,768]{2,1,0:T(8,128)(2,1)S(1)} %collective-permute-done.17) | copy-start | bytes 884740
  263.9 3.7 %collective-permute-start.19 = (bf16[4,240,768]{2,1,0:T(8,128)(2,1)}, bf16[4,240,768]{2,1,0:T(8,128)(2,1)}, u32[]{:S(2)}, u32[]{:S(2)}) collective-permute-start(bf16[4,240,768]{2,1,0:T(8,128)(2,1)} %get-tuple-element.186), channel_id=1, source_target_pairs={{0,1},{1,0},{2,3},{3,2},{4,5},{5,4},{6,7},{7,6},{8,9},{9,8},{10,11... | collective-permute-start | bytes 4423688 | tf_op jit(solution)/shard_map/ppermute | solution.py:958
  264.2 21.1 %collective-permute-start.24 = (bf16[4,240,768]{2,1,0:T(8,128)(2,1)}, bf16[4,240,768]{2,1,0:T(8,128)(2,1)}, u32[]{:S(2)}, u32[]{:S(2)}) collective-permute-start(bf16[4,240,768]{2,1,0:T(8,128)(2,1)} %copy-done.17), channel_id=1, source_target_pairs={{0,1},{1,0},{2,3},{3,2},{4,5},{5,4},{6,7},{7,6},{8,9},{9,8},{10,11... | collective-permute-start | bytes 4423688 | tf_op jit(solution)/shard_map/ppermute | solution.py:958
  267.7 14.5 %collective-permute-start.32 = (bf16[96,768]{1,0:T(8,128)(2,1)}, bf16[96,768]{1,0:T(8,128)(2,1)}, u32[]{:S(2)}, u32[]{:S(2)}) collective-permute-start(bf16[96,768]{1,0:T(8,128)(2,1)} %fusion.17), channel_id=1, source_target_pairs={{0,2},{1,3},{2,0},{3,1},{4,6},{5,7},{6,4},{7,5},{8,10},{9,11},{10,... | collective-permute-start | bytes 442376 | tf_op jit(solution)/shard_map/ppermute | solution.py:958
  268.5 6.5 %copy-start.20 = (bf16[4,240,768]{2,1,0:T(8,128)(2,1)S(1)}, bf16[4,240,768]{2,1,0:T(8,128)(2,1)}, u32[]{:S(2)}) copy-start(bf16[4,240,768]{2,1,0:T(8,128)(2,1)} %get-tuple-element.170) | copy-start | bytes 4423684
  268.5 5.9 %collective-permute-start.25 = (bf16[1,3,4608]{2,1,0:T(4,128)(2,1)S(1)}, bf16[1,3,4608]{2,1,0:T(4,128)(2,1)S(1)}, u32[]{:S(2)}, u32[]{:S(2)}) collective-permute-start(bf16[1,3,4608]{2,1,0:T(4,128)(2,1)S(1)} %pad_maximum_fusion.6), channel_id=1, source_target_pairs={{0,8},{1,9},{2,10},{3,11},{4,12},{5,13},{6,14},{7,15},{8,0},{9,1},... | collective-permute-start | bytes 82952 | tf_op jit(solution)/shard_map/ppermute | solution.py:958
  272.9 39.9 %collective-permute-start.23 = (bf16[4,240,768]{2,1,0:T(8,128)(2,1)}, bf16[4,240,768]{2,1,0:T(8,128)(2,1)S(1)}, u32[]{:S(2)}, u32[]{:S(2)}) collective-permute-start(bf16[4,240,768]{2,1,0:T(8,128)(2,1)} %add_convert_fusion), channel_id=1, source_target_pairs={{0,2},{1,3},{2,0},{3,1},{4,6},{5,7},{6,4},{7,5},{8,10},{9,11},{10,... | collective-permute-start | bytes 4423688 | tf_op jit(solution)/shard_map/ppermute | solution.py:958
  274.5 6.1 %collective-permute-start.26 = (bf16[2,3,4608]{2,1,0:T(4,128)(2,1)S(1)}, bf16[2,3,4608]{2,1,0:T(4,128)(2,1)S(1)}, u32[]{:S(2)}, u32[]{:S(2)}) collective-permute-start(bf16[2,3,4608]{2,1,0:T(4,128)(2,1)S(1)} %maximum_bitcast_fusion.2), channel_id=1, source_target_pairs={{0,4},{1,5},{2,6},{3,7},{4,0},{5,1},{6,2},{7,3},{8,12},{9,13},{10,... | collective-permute-start | bytes 165896 | tf_op jit(solution)/shard_map/ppermute | solution.py:958
  278.2 13.7 %collective-permute-start.20 = (bf16[240,768]{1,0:T(8,128)(2,1)}, bf16[240,768]{1,0:T(8,128)(2,1)}, u32[]{:S(2)}, u32[]{:S(2)}) collective-permute-start(bf16[240,768]{1,0:T(8,128)(2,1)} %get-tuple-element.233), channel_id=1, source_target_pairs={{0,12},{1,13},{2,14},{3,15},{4,8},{5,9},{6,10},{7,11},{8,4},{9,5},... | collective-permute-start | bytes 1105928 | tf_op jit(solution)/shard_map/ppermute | solution.py:958
  280.6 32.1 %collective-permute-start.21 = (bf16[240,768]{1,0:T(8,128)(2,1)}, bf16[240,768]{1,0:T(8,128)(2,1)}, u32[]{:S(2)}, u32[]{:S(2)}) collective-permute-start(bf16[240,768]{1,0:T(8,128)(2,1)} %get-tuple-element.232), channel_id=1, source_target_pairs={{0,8},{1,9},{2,10},{3,11},{4,12},{5,13},{6,14},{7,15},{8,0},{9,1},... | collective-permute-start | bytes 1105928 | tf_op jit(solution)/shard_map/ppermute | solution.py:958
  282.2 30.5 %collective-permute-start.22 = (bf16[240,768]{1,0:T(8,128)(2,1)}, bf16[240,768]{1,0:T(8,128)(2,1)S(1)}, u32[]{:S(2)}, u32[]{:S(2)}) collective-permute-start(bf16[240,768]{1,0:T(8,128)(2,1)} %get-tuple-element.231), channel_id=1, source_target_pairs={{0,4},{1,5},{2,6},{3,7},{4,0},{5,1},{6,2},{7,3},{8,12},{9,13},{10,... | collective-permute-start | bytes 1105928 | tf_op jit(solution)/shard_map/ppermute | solution.py:958
  312.7 7.5 %copy-start.19 = (bf16[4,240,768]{2,1,0:T(8,128)(2,1)}, bf16[4,240,768]{2,1,0:T(8,128)(2,1)S(1)}, u32[]{:S(2)}) copy-start(bf16[4,240,768]{2,1,0:T(8,128)(2,1)S(1)} %collective-permute-done.23) | copy-start | bytes 4423684
  312.7 7.5 %copy-start.28 = (bf16[4,3,4608]{2,0,1:T(4,128)(2,1)S(1)}, bf16[4,3,4608]{2,0,1:T(4,128)(2,1)}, u32[]{:S(2)}) copy-start(bf16[4,3,4608]{2,0,1:T(4,128)(2,1)} %reshape.214) | copy-start | bytes 331780
  315.8 13.7 %collective-permute-start.29 = (bf16[240,768]{1,0:T(8,128)(2,1)}, bf16[240,768]{1,0:T(8,128)(2,1)}, u32[]{:S(2)}, u32[]{:S(2)}) collective-permute-start(bf16[240,768]{1,0:T(8,128)(2,1)} %get-tuple-element.228), channel_id=1, source_target_pairs={{0,12},{1,13},{2,14},{3,15},{4,8},{5,9},{6,10},{7,11},{8,4},{9,5},... | collective-permute-start | bytes 1105928 | tf_op jit(solution)/shard_map/ppermute | solution.py:958
  317.0 30.3 %collective-permute-start.30 = (bf16[240,768]{1,0:T(8,128)(2,1)}, bf16[240,768]{1,0:T(8,128)(2,1)}, u32[]{:S(2)}, u32[]{:S(2)}) collective-permute-start(bf16[240,768]{1,0:T(8,128)(2,1)} %get-tuple-element.230), channel_id=1, source_target_pairs={{0,8},{1,9},{2,10},{3,11},{4,12},{5,13},{6,14},{7,15},{8,0},{9,1},... | collective-permute-start | bytes 1105928 | tf_op jit(solution)/shard_map/ppermute | solution.py:958
  317.0 30.3 %collective-permute-start.31 = (bf16[240,768]{1,0:T(8,128)(2,1)}, bf16[240,768]{1,0:T(8,128)(2,1)}, u32[]{:S(2)}, u32[]{:S(2)}) collective-permute-start(bf16[240,768]{1,0:T(8,128)(2,1)} %get-tuple-element.229), channel_id=1, source_target_pairs={{0,4},{1,5},{2,6},{3,7},{4,0},{5,1},{6,2},{7,3},{8,12},{9,13},{10,... | collective-permute-start | bytes 1105928 | tf_op jit(solution)/shard_map/ppermute | solution.py:958
  320.2 4.7 %collective-permute-start.27 = (bf16[4,3,4608]{2,0,1:T(4,128)(2,1)S(1)}, bf16[4,3,4608]{2,0,1:T(4,128)(2,1)S(1)}, u32[]{:S(2)}, u32[]{:S(2)}) collective-permute-start(bf16[4,3,4608]{2,0,1:T(4,128)(2,1)S(1)} %copy-done.28), channel_id=1, source_target_pairs={{0,2},{1,3},{2,0},{3,1},{4,6},{5,7},{6,4},{7,5},{8,10},{9,11},{10,... | collective-permute-start | bytes 331784 | tf_op jit(solution)/shard_map/ppermute | solution.py:958
  325.5 1.5 collective-permute-start.28
  (6 other events, 6.6 us)
Sparse Core Ops, SparseCore 0:
  10.9 116.6 all-gather.2
